TPU v7x, 512 devices: a whole 4x4x16 slice. The times are simulated.
512 devices in a mesh: dp: 32 (over z, core), space: 16 (over x, y).
Axes of the slice: x: 4, y: 4, z: 16, core: 2. Of those that a mesh axis runs over, the one named last changes fastest.
Arguments:
- inputs: bfloat16 [32, 256, 9216], P('dp', 'space'), may hold values from -6 to 6
- cotangent: bfloat16 [32, 256, 9216], P('dp', 'space'), may hold values from -6 to 6
- weights: bfloat16 [3, 9, 36864], replicated, may hold values from -0.15625 to 0.15625
Outputs:
- outputs: bfloat16 [32, 256, 9216], P('dp', 'space')
- input_grad: bfloat16 [32, 256, 9216], P('dp', 'space')
- weight_grad: float32 [27, 36864], P(None, ('dp', 'space'))
All inputs are finite; a program needn't handle non-finite values.
Results may differ from a plain program's by a relative error of at most 0.014.
Values may be sent and summed in bfloat16 or wider, within the bound.
No kernel may reach another device: no remote copies, remote signals or barrier semaphores. Data moves between devices by JAX's collectives and lax.ppermute only.
A program may use at most 128 MiB of HBM per device.

v0:
```python
import math

import jax
import jax.numpy as jnp
from jax import lax
from jax.sharding import PartitionSpec as P

CHANNELS = 192
LAYERS = 3


def padded_2(value, sides, width):
    for axis, dim in sides:
        count, length = (lax.axis_size(axis), value.shape[dim])
        up = [(i, (i + 1) % count) for i in range(count - 1)]
        down = [(j, i) for i, j in up]
        last = lax.slice_in_dim(value, length - width, length, axis=dim)
        leading = lax.slice_in_dim(value, 0, width, axis=dim)
        before = lax.ppermute(last, axis, up)
        after = lax.ppermute(leading, axis, down)
        value = jnp.concatenate([before, value, after], axis=dim)
    return value


def passed_along(value, axis, by):
    count = lax.axis_size(axis)
    pairs = [(i, i + by) for i in range(count) if 0 <= i + by < count]
    return lax.ppermute(value, axis, pairs)


def column_slide(values, offset):
    if offset == 0:
        return values
    filler = jnp.zeros((values.shape[0], abs(offset)) + values.shape[2:], values.dtype)
    if offset > 0:
        return jnp.concatenate([values[:, offset:], filler], 1)
    return jnp.concatenate([filler, values[:, :offset]], 1)


def tap_columns(around, spread, flipped):
    channel_count = around[1].shape[-1]
    pieces = []
    for i in range(3):
        for j in range(3):
            if flipped:
                pieces.append(column_slide(around[2 - i], (1 - j) * spread))
            else:
                pieces.append(column_slide(around[i], (j - 1) * spread))
    return jnp.concatenate(pieces, -1).reshape(-1, 9 * channel_count)


def kernel_grad(stacked_cols, upstream):
    channel_count = upstream.shape[-1]
    flat_up = upstream.reshape(-1, channel_count)
    product = lax.dot_general(
        stacked_cols, flat_up, (((0,), (0,)), ((), ())), preferred_element_type=jnp.float32
    )
    return product.reshape(9, channel_count * channel_count)


def gelu_slope(values):
    return jax.vjp(jax.nn.gelu, values)[1](jnp.ones_like(values))[0]


def activate(values):
    return jax.nn.gelu(values.astype(jnp.float32)).astype(jnp.bfloat16)


def body(inputs, cotangent, weights):
    rows_here = inputs.shape[1]
    flat_width = inputs.shape[2]
    columns = flat_width // CHANNELS
    shape_three = (rows_here, columns, CHANNELS)
    kernels = weights.reshape(LAYERS, 9, CHANNELS, CHANNELS)
    forward_stack = kernels.reshape(LAYERS, 9 * CHANNELS, CHANNELS)
    backward_stack = jnp.transpose(kernels, (0, 1, 3, 2)).reshape(LAYERS, 9 * CHANNELS, CHANNELS)
    spaces = lax.axis_size("space")
    grad_scale = 1.0 / math.sqrt(lax.axis_size("dp") * spaces * rows_here * columns)

    def flatten(values):
        return values.reshape(rows_here, flat_width)

    def unflatten(values):
        return values.reshape(shape_three)

    def advance(current, around, layer_index, spread):
        stacked_cols = tap_columns(around, spread, False)
        branch = jnp.dot(
            stacked_cols, forward_stack[layer_index], preferred_element_type=jnp.float32
        )
        branch = branch.reshape(shape_three)
        return ((current.astype(jnp.float32) + branch).astype(jnp.bfloat16), stacked_cols)

    def retreat(upstream, around, current, layer_index, spread):
        stacked_cols = tap_columns(around, spread, True)
        backward_term = jnp.dot(
            stacked_cols, backward_stack[layer_index], preferred_element_type=jnp.float32
        )
        backward_term = backward_term.reshape(shape_three)
        slope = gelu_slope(current.astype(jnp.float32))
        return (upstream.astype(jnp.float32) + backward_term * slope).astype(jnp.bfloat16)

    state_zero = inputs.reshape(shape_three)
    active_zero = activate(state_zero)
    padded = padded_2(flatten(active_zero), (("space", 0),), 1)
    padded = padded.reshape(rows_here + 2, columns, CHANNELS)
    around_zero = (padded[:-2], active_zero, padded[2:])
    state_one, cols_zero = advance(state_zero, around_zero, 0, 1)
    upstream = cotangent.reshape(rows_here, flat_width)
    active_one = activate(state_one)
    above = unflatten(passed_along(flatten(active_one), "space", 1))
    below = unflatten(passed_along(flatten(active_one), "space", -1))
    around_one = (above, active_one, below)
    state_two, cols_one = advance(state_one, around_one, 1, rows_here)
    active_two = activate(state_two)
    far_above = unflatten(passed_along(flatten(active_two), "space", 2))
    far_below = unflatten(passed_along(flatten(active_two), "space", -2))
    around_two = (far_above, active_two, far_below)
    state_three, cols_two = advance(state_two, around_two, 2, 2 * rows_here)
    final_state = flatten(state_three)
    outputs = final_state.reshape(1, rows_here, flat_width)
    grad_three = unflatten(upstream)
    grad_far_above = unflatten(passed_along(upstream, "space", 2))
    grad_far_below = unflatten(passed_along(upstream, "space", -2))
    around_grad = (grad_far_above, grad_three, grad_far_below)
    term_two = kernel_grad(cols_two, grad_three)
    grad_two = retreat(grad_three, around_grad, state_two, 2, 2 * rows_here)
    grad_upper = unflatten(passed_along(flatten(grad_two), "space", 1))
    grad_lower = unflatten(passed_along(flatten(grad_two), "space", -1))
    term_one = kernel_grad(cols_one, grad_two)
    grad_one = retreat(grad_two, (grad_upper, grad_two, grad_lower), state_one, 1, rows_here)
    padded_grad = padded_2(flatten(grad_one), (("space", 0),), 1)
    padded_grad = padded_grad.reshape(rows_here + 2, columns, CHANNELS)
    term_zero = kernel_grad(cols_zero, grad_one)
    grad_zero = retreat(grad_one, (padded_grad[:-2], grad_one, padded_grad[2:]), state_zero, 0, 1)
    input_grad = grad_zero.reshape(1, rows_here, flat_width)
    stacked = jnp.concatenate([term_zero, term_one, term_two], 0) * grad_scale
    weight_grad = lax.psum_scatter(stacked, ("dp", "space"), scatter_dimension=1, tiled=True)
    return (outputs, input_grad, weight_grad)


def solution(mesh):
    placed = (P("dp", "space", None), P("dp", "space", None), P())
    return jax.shard_map(
        body,
        mesh=mesh,
        in_specs=placed,
        out_specs=(P("dp", "space", None), P("dp", "space", None), P(None, ("dp", "space"))),
        check_vma=False,
    )
```

profile of v0, /device:TPU:2, one launch (start us, length us, event | category | flops | bytes accessed | tf_op | source)
XLA Modules:
  0.0 716.2 jit_solution(12555101030037358242)
XLA Ops:
  7.2 5.2 collective-permute-start.6
  12.4 2.3 collective-permute-start.7
  18.4 5.8 collective-permute-start.1
  30.6 10.5 %slice_reduce_fusion = (bf16[9,36864]{1,0:T(8,128)(2,1)}, bf16[9,36864]{1,0:T(8,128)(2,1)}, bf16[9,36864]{1,0:T(8,128)(2,1)}) fusion(bf16[3,9,36864]{2,0,1:T(4,128)(2,1)S(1)} %copy-done), kind=kLoop, calls=%fused_computation.15 | loop fusion | bytes 3981312 | tf_op jit(solution)/shard_map/slice | solution.py:89
  41.1 4.0 reshape.298
  45.1 4.1 copy.20
  57.5 2.9 squeeze.18
  71.7 5.6 concatenate.183
  77.3 3.7 fusion.25
  84.2 6.1 collective-permute-start.3
  96.5 5.3 concatenate.204
  105.0 3.4 concatenate.190
  108.4 3.2 fusion.30
  112.7 3.4 collective-permute-start.4
  116.1 4.8 collective-permute-start.5
  120.9 3.0 fusion.4
  125.1 3.7 collective-permute-start.8
  130.9 3.9 convolution_bitcast_fusion
  138.1 2.7 reshape.305
  148.8 5.6 concatenate.211
  154.4 3.4 add_convert_fusion
  165.5 2.2 reshape.294
  175.3 6.0 collective-permute-start.10
  181.4 5.6 concatenate.197
  191.3 5.6 concatenate.230
  196.9 4.0 fusion.61
  201.0 3.7 reshape.306
  204.7 3.7 reshape.304
  208.4 5.3 maximum_multiply_fusion
  223.6 5.1 concatenate.220
  228.7 3.2 fusion.3
  233.0 474.4 %all-reduce.39.cloned.1.call-done = f32[27,36864]{1,0:T(8,128)} async-done(((f32[27,36864]{1,0:T(8,128)}), f32[27,36864]{1,0:T(8,128)}) %all-reduce.39.cloned.1.call-update) | async-done | bytes 3981328
  (136 shorter events, 89.6 us)
Async XLA Ops:
  7.2 23.5 %copy-start = (bf16[3,9,36864]{2,0,1:T(4,128)(2,1)S(1)}, bf16[3,9,36864]{2,0,1:T(4,128)(2,1)}, u32[]{:S(2)}) copy-start(bf16[3,9,36864]{2,0,1:T(4,128)(2,1)} %param.5) | copy-start | bytes 5971972
  7.2 700.3 %all-reduce.39.cloned.1.call-start = ((), (), s32[]{:S(2)}) async-start(), calls=%async_computation | async-start | bytes 9437184
  7.2 83.2 %collective-permute-start.6 = (bf16[16,9216]{1,0:T(8,128)(2,1)}, bf16[16,9216]{1,0:T(8,128)(2,1)}, u32[]{:S(2)}, u32[]{:S(2)}) collective-permute-start(bf16[16,9216]{1,0:T(8,128)(2,1)} %bitcast.64), channel_id=1, source_target_pairs={{2,0},{3,1},{4,2},{5,3},{6,4},{7,5},{8,6},{9,7},{10,8},{11,9},{12,... | collective-permute-start | bytes 884744 | tf_op jit(solution)/shard_map/ppermute | solution.py:28
  12.4 79.5 %collective-permute-start.7 = (bf16[16,9216]{1,0:T(8,128)(2,1)}, bf16[16,9216]{1,0:T(8,128)(2,1)}, u32[]{:S(2)}, u32[]{:S(2)}) collective-permute-start(bf16[16,9216]{1,0:T(8,128)(2,1)} %bitcast.65), channel_id=1, source_target_pairs={{0,2},{1,3},{2,4},{3,5},{4,6},{5,7},{6,8},{7,9},{8,10},{9,11},{10,... | collective-permute-start | bytes 884744 | tf_op jit(solution)/shard_map/ppermute | solution.py:28
  18.4 47.4 %collective-permute-start.1 = (bf16[1,9216]{1,0:T(2,128)(2,1)S(1)}, bf16[1,9216]{1,0:T(2,128)(2,1)S(1)}, u32[]{:S(2)}, u32[]{:S(2)}) collective-permute-start(bf16[1,9216]{1,0:T(2,128)(2,1)S(1)} %slice.193), channel_id=1, source_target_pairs={{1,0},{2,1},{3,2},{4,3},{5,4},{6,5},{7,6},{8,7},{9,8},{10,9},{11,1... | collective-permute-start | bytes 55304 | tf_op jit(solution)/shard_map/ppermute | solution.py:20
  24.3 41.5 %collective-permute-start = (bf16[1,9216]{1,0:T(2,128)(2,1)S(1)}, bf16[1,9216]{1,0:T(2,128)(2,1)}, u32[]{:S(2)}, u32[]{:S(2)}) collective-permute-start(bf16[1,9216]{1,0:T(2,128)(2,1)S(1)} %slice.185), channel_id=1, source_target_pairs={{0,1},{1,2},{2,3},{3,4},{4,5},{5,6},{6,7},{7,8},{8,9},{9,10},{10,1... | collective-permute-start | bytes 55304 | tf_op jit(solution)/shard_map/ppermute | solution.py:19
  30.6 65.9 %copy-start.6 = (bf16[16,48,192]{2,1,0:T(8,128)(2,1)}, bf16[16,48,192]{2,1,0:T(8,128)(2,1)S(1)}, u32[]{:S(2)}) copy-start(bf16[16,48,192]{2,1,0:T(8,128)(2,1)S(1)} %reshape_reshape.8) | copy-start | bytes 884740
  50.8 9.6 %copy-start.2 = (bf16[9,36864]{1,0:T(8,128)(2,1)S(1)}, bf16[9,36864]{1,0:T(8,128)(2,1)}, u32[]{:S(2)}) copy-start(bf16[9,36864]{1,0:T(8,128)(2,1)} %get-tuple-element.4) | copy-start | bytes 1990660
  53.7 8.5 %copy-start.1 = (bf16[9,36864]{1,0:T(8,128)(2,1)S(1)}, bf16[9,36864]{1,0:T(8,128)(2,1)}, u32[]{:S(2)}) copy-start(bf16[9,36864]{1,0:T(8,128)(2,1)} %get-tuple-element.3) | copy-start | bytes 1990660
  60.4 5.5 copy-start.10
  71.7 5.6 copy-start.4
  82.1 19.7 %collective-permute-start.2 = (bf16[16,9216]{1,0:T(8,128)(2,1)}, bf16[16,9216]{1,0:T(8,128)(2,1)}, u32[]{:S(2)}, u32[]{:S(2)}) collective-permute-start(bf16[16,9216]{1,0:T(8,128)(2,1)} %reshape.289), channel_id=1, source_target_pairs={{0,1},{1,2},{2,3},{3,4},{4,5},{5,6},{6,7},{7,8},{8,9},{9,10},{10,1... | collective-permute-start | bytes 884744 | tf_op jit(solution)/shard_map/ppermute | solution.py:28
  84.2 19.2 %collective-permute-start.3 = (bf16[16,9216]{1,0:T(8,128)(2,1)}, bf16[16,9216]{1,0:T(8,128)(2,1)}, u32[]{:S(2)}, u32[]{:S(2)}) collective-permute-start(bf16[16,9216]{1,0:T(8,128)(2,1)} %reshape.289), channel_id=1, source_target_pairs={{1,0},{2,1},{3,2},{4,3},{5,4},{6,5},{7,6},{8,7},{9,8},{10,9},{11,1... | collective-permute-start | bytes 884744 | tf_op jit(solution)/shard_map/ppermute | solution.py:28
  108.3 12.6 %copy-start.7 = (bf16[16,48,192]{2,1,0:T(8,128)(2,1)S(1)}, bf16[16,48,192]{2,1,0:T(8,128)(2,1)}, u32[]{:S(2)}) copy-start(bf16[16,48,192]{2,1,0:T(8,128)(2,1)} %copy-done.6) | copy-start | bytes 884740
  108.3 12.6 %copy-start.11 = (bf16[1,9,192,192]{3,2,1,0:T(8,128)(2,1)S(1)}, bf16[1,9,192,192]{3,2,1,0:T(8,128)(2,1)}, u32[]{:S(2)}) copy-start(bf16[1,9,192,192]{3,2,1,0:T(8,128)(2,1)} %get-tuple-element.8) | copy-start | bytes 1990660
  111.6 12.4 %copy-start.12 = (bf16[16,48,192]{2,1,0:T(8,128)(2,1)}, bf16[16,48,192]{2,1,0:T(8,128)(2,1)S(1)}, u32[]{:S(2)}) copy-start(bf16[16,48,192]{2,1,0:T(8,128)(2,1)S(1)} %get-tuple-element.56) | copy-start | bytes 884740
  112.7 47.4 %collective-permute-start.4 = (bf16[16,9216]{1,0:T(8,128)(2,1)}, bf16[16,9216]{1,0:T(8,128)(2,1)}, u32[]{:S(2)}, u32[]{:S(2)}) collective-permute-start(bf16[16,9216]{1,0:T(8,128)(2,1)} %reshape.292), channel_id=1, source_target_pairs={{0,2},{1,3},{2,4},{3,5},{4,6},{5,7},{6,8},{7,9},{8,10},{9,11},{10,... | collective-permute-start | bytes 884744 | tf_op jit(solution)/shard_map/ppermute | solution.py:28
  116.1 49.4 %collective-permute-start.5 = (bf16[16,9216]{1,0:T(8,128)(2,1)}, bf16[16,9216]{1,0:T(8,128)(2,1)}, u32[]{:S(2)}, u32[]{:S(2)}) collective-permute-start(bf16[16,9216]{1,0:T(8,128)(2,1)} %reshape.292), channel_id=1, source_target_pairs={{2,0},{3,1},{4,2},{5,3},{6,4},{7,5},{8,6},{9,7},{10,8},{11,9},{12,... | collective-permute-start | bytes 884744 | tf_op jit(solution)/shard_map/ppermute | solution.py:28
  125.1 15.7 %collective-permute-start.8 = (bf16[16,9216]{1,0:T(8,128)(2,1)}, bf16[16,9216]{1,0:T(8,128)(2,1)}, u32[]{:S(2)}, u32[]{:S(2)}) collective-permute-start(bf16[16,9216]{1,0:T(8,128)(2,1)} %reshape.299), channel_id=1, source_target_pairs={{1,0},{2,1},{3,2},{4,3},{5,4},{6,5},{7,6},{8,7},{9,8},{10,9},{11,1... | collective-permute-start | bytes 884744 | tf_op jit(solution)/shard_map/ppermute | solution.py:28
  128.8 15.1 %collective-permute-start.9 = (bf16[16,9216]{1,0:T(8,128)(2,1)}, bf16[16,9216]{1,0:T(8,128)(2,1)}, u32[]{:S(2)}, u32[]{:S(2)}) collective-permute-start(bf16[16,9216]{1,0:T(8,128)(2,1)} %reshape.299), channel_id=1, source_target_pairs={{0,1},{1,2},{2,3},{3,4},{4,5},{5,6},{6,7},{7,8},{8,9},{9,10},{10,1... | collective-permute-start | bytes 884744 | tf_op jit(solution)/shard_map/ppermute | solution.py:28
  154.4 3.5 copy-start.8
  160.0 21.3 %copy-start.3 = (bf16[16,48,192]{2,1,0:T(8,128)(2,1)S(1)}, bf16[16,48,192]{2,1,0:T(8,128)(2,1)}, u32[]{:S(2)}) copy-start(bf16[16,48,192]{2,1,0:T(8,128)(2,1)} %concatenate.193) | copy-start | bytes 884740
  171.7 47.7 %collective-permute-start.11 = (bf16[1,9216]{1,0:T(2,128)(2,1)}, bf16[1,9216]{1,0:T(2,128)(2,1)}, u32[]{:S(2)}, u32[]{:S(2)}) collective-permute-start(bf16[1,9216]{1,0:T(2,128)(2,1)} %slice.236), channel_id=1, source_target_pairs={{0,1},{1,2},{2,3},{3,4},{4,5},{5,6},{6,7},{7,8},{8,9},{9,10},{10,1... | collective-permute-start | bytes 55304 | tf_op jit(solution)/shard_map/ppermute | solution.py:19
  175.3 44.1 %collective-permute-start.10 = (bf16[1,9216]{1,0:T(2,128)(2,1)}, bf16[1,9216]{1,0:T(2,128)(2,1)}, u32[]{:S(2)}, u32[]{:S(2)}) collective-permute-start(bf16[1,9216]{1,0:T(2,128)(2,1)} %slice.228), channel_id=1, source_target_pairs={{1,0},{2,1},{3,2},{4,3},{5,4},{6,5},{7,6},{8,7},{9,8},{10,9},{11,1... | collective-permute-start | bytes 55304 | tf_op jit(solution)/shard_map/ppermute | solution.py:20
  213.6 1.8 copy-start.9
  223.6 5.1 copy-start.5
Sparse Core Ops, SparseCore 0:
  213.8 493.6 all-reduce.38
where the time goes:
time: 722 us; the launch traced here: 716 us
  waiting for transfers between devices  474 us (66%)
  local copies, waits for them, and re-layouts  142 us (20%)
  starting transfers between devices  45.6 us (6%)
  matrix products  28.8 us (4%)
  between operations  15 us (2%)
  other arithmetic  10.5 us (1%)
    unnamed x2, waiting for transfers between devices  474 us
    concatenate x9, local copies, waits for them, and re-layouts, tap_columns(): return jnp.concatenate(pieces, -1).reshape(-1, 9 * channel_count)  40.6 us
    ppermute x8, starting transfers between devices, passed_along(): return lax.ppermute(value, axis, pairs)  29.7 us
  transfers between devices with their start and end apart: 13, of which 1 were waited for; matrix products, arithmetic and copies ran while one was open for 23% of the time, Pallas kernels for 0%

commit v1 on v0

v1 whole, which is shorter than its diff:
```python
import math

import jax
import jax.numpy as jnp
from jax import lax
from jax.experimental import pallas as pl
from jax.experimental.pallas import tpu as pltpu
from jax.sharding import Mesh
from jax.sharding import PartitionSpec as P


DP = ("z", "core")
SPACE = ("x", "y")
CH = 192
ROWS = 16
WIDTH = 48
HEIGHT = 256
GROUPS = 3
CELLS = GROUPS * HEIGHT
F32 = jnp.float32
BF16 = jnp.bfloat16
GELU_A = math.sqrt(2.0 / math.pi)
GELU_B = 0.044715
VMEM_LIMIT = 24 * 1024 * 1024


def gelu(x):
    return x * (0.5 * (1.0 + jnp.tanh(GELU_A * (x + GELU_B * (x * x * x)))))


def gelu_and_slope(x):
    square = x * x
    tanh = jnp.tanh(GELU_A * (x + GELU_B * (x * square)))
    cdf = 0.5 * (1.0 + tanh)
    slope = cdf + (0.5 * x) * ((1.0 - tanh * tanh) * (GELU_A + (3.0 * GELU_A * GELU_B) * square))
    return x * cdf, slope


def dot(a, b):
    return lax.dot_general(a, b, (((1,), (0,)), ((), ())), preferred_element_type=F32)


def dot_t(a, b):
    return lax.dot_general(a, b, (((1,), (1,)), ((), ())), preferred_element_type=F32)


def call(kernel, out_shape, *args, scratch=(), flops=0, moved=0, after=()):
    return pl.pallas_call(
        kernel,
        out_shape=out_shape,
        in_specs=[pl.BlockSpec(memory_space=pltpu.VMEM)] * len(args)
        + [pl.BlockSpec(memory_space=pl.ANY)] * len(after),
        out_specs=jax.tree.map(lambda _: pl.BlockSpec(memory_space=pltpu.VMEM), out_shape),
        scratch_shapes=list(scratch),
        compiler_params=pltpu.CompilerParams(vmem_limit_bytes=VMEM_LIMIT),
        cost_estimate=pl.CostEstimate(flops=flops, bytes_accessed=moved, transcendentals=0),
    )(*args, *after)


def shape(*dims, dtype=BF16):
    return jax.ShapeDtypeStruct(dims, dtype)


def pack_kernel(x_hbm, c_hbm, send_ref, x_ref, c_ref, act_ref, sems):
    copies = [
        pltpu.make_async_copy(x_hbm, x_ref, sems.at[0]),
        pltpu.make_async_copy(c_hbm, c_ref, sems.at[1]),
    ]
    for copy in copies:
        copy.start()
    for copy in copies:
        copy.wait()
    act_ref[...] = gelu(x_ref[0].astype(F32)).astype(BF16)

    def column(load, w):
        pair = load(384 * (w // 2))
        base = 192 * (w % 2)
        return pair[:, base : base + 128], pair[:, base + 128 : base + 192]

    nothing = jnp.zeros((16, 128), BF16), jnp.zeros((16, 64), BF16)
    act, raw, cot = [], [], []
    for w in range(WIDTH):
        act.append(column(lambda at: act_ref[:, at : at + 384], w))
        raw.append(column(lambda at: x_ref[0, :, at : at + 384], w))
        cot.append(column(lambda at: c_ref[0, :, at : at + 384], w))
    for b in range(16):
        blocks = []
        for g in range(4):
            for a in range(GROUPS):
                w = 16 * a + b
                if g == 0:
                    blocks.append(act[w - 1] if w > 0 else nothing)
                elif g == 1:
                    blocks.append(raw[w])
                elif g == 2:
                    blocks.append(act[w + 1] if w < WIDTH - 1 else nothing)
                else:
                    blocks.append(cot[w])
        for k in range(12):
            send_ref[b, 16 * k : 16 * k + 16, :] = blocks[k][0]
        for k in range(6):
            both = jnp.concatenate([blocks[2 * k][1], blocks[2 * k + 1][1]], axis=1)
            send_ref[b, 192 + 16 * k : 208 + 16 * k, :] = both


def shifted_rows(value, by):
    rows = lax.broadcasted_iota(jnp.int32, value.shape, 0)
    rolled = pltpu.roll(value, (-by) % value.shape[0], 0)
    keep = rows != (0 if by < 0 else value.shape[0] - 1)
    return jnp.where(keep, rolled, 0.0)


def spread_conv(padded, w_ref, layer, width, step, transposed):
    totals = [None] * GROUPS
    for j in range(3):
        off = (1 - j) * step if transposed else (j - 1) * step
        outs = [a for a in range(GROUPS) if 0 <= a + off < GROUPS]
        lo, n = outs[0], len(outs)
        total = None
        for i in range(3):
            at = width * (2 - i) if transposed else width * i
            cells = padded[lo + off : lo + off + n, at : at + HEIGHT, :].reshape(n * HEIGHT, CH)
            kernel = w_ref[9 * layer + 3 * i + j]
            term = dot_t(cells, kernel) if transposed else dot(cells, kernel)
            total = term if total is None else total + term
        for m, a in enumerate(outs):
            part = total[m * HEIGHT : (m + 1) * HEIGHT]
            totals[a] = part if totals[a] is None else totals[a] + part
    return totals


def clear_edges(ref, pad):
    for a in range(GROUPS):
        ref[a, 0:pad, :] = jnp.zeros((pad, CH), BF16)
        ref[a, pad + HEIGHT : 2 * pad + HEIGHT, :] = jnp.zeros((pad, CH), BF16)


def main_kernel(
    recv_ref, w_ref, a0_ref, a1_ref, a2_ref, g1_ref, g2_ref, g3_ref, s2_ref,
    a1p, g2p, g3p, slope1, slope2,
):
    def block(k):
        lo = recv_ref[:, 16 * k : 16 * k + 16, :].reshape(HEIGHT, 128)
        at = 192 + 16 * (k // 2)
        hi = recv_ref[:, at : at + 16, :].reshape(HEIGHT, 128)[:, 64 * (k % 2) : 64 * (k % 2) + 64]
        return jnp.concatenate([lo, hi], axis=1)

    for ref, pad in ((a1p, 16), (g2p, 16), (g3p, 32)):
        clear_edges(ref, pad)

    state = []
    for a in range(GROUPS):
        rows = slice(HEIGHT * a, HEIGHT * (a + 1))
        a0_ref[0, rows, :] = block(a)
        raw = block(3 + a)
        state.append(raw)
        a0_ref[1, rows, :] = gelu(raw.astype(F32)).astype(BF16)
        a0_ref[2, rows, :] = block(6 + a)
        cot = block(9 + a)
        g3_ref[rows, :] = cot
        g3p[a, 32 : 32 + HEIGHT, :] = cot

    sums = []
    for i in range(3):
        total = None
        for j in range(3):
            term = dot(a0_ref[j], w_ref[3 * i + j])
            total = term if total is None else total + term
        sums.append(total)
    for a in range(GROUPS):
        rows = slice(HEIGHT * a, HEIGHT * (a + 1))
        branch = shifted_rows(sums[0][rows], -1) + sums[1][rows] + shifted_rows(sums[2][rows], 1)
        state[a] = (state[a].astype(F32) + branch).astype(BF16)
        act, slope = gelu_and_slope(state[a].astype(F32))
        act = act.astype(BF16)
        slope1[rows, :] = slope
        a1_ref[rows, :] = act
        a1p[a, 16 : 16 + HEIGHT, :] = act

    branch = spread_conv(a1p, w_ref, 1, 16, 1, False)
    for a in range(GROUPS):
        rows = slice(HEIGHT * a, HEIGHT * (a + 1))
        state[a] = (state[a].astype(F32) + branch[a]).astype(BF16)
        act, slope = gelu_and_slope(state[a].astype(F32))
        act = act.astype(BF16)
        slope2[rows, :] = slope
        a2_ref[rows, :] = act
        s2_ref[rows, :] = state[a]

    back = spread_conv(g3p, w_ref, 2, 32, 2, True)
    for a in range(GROUPS):
        rows = slice(HEIGHT * a, HEIGHT * (a + 1))
        grad = g3_ref[rows, :].astype(F32) + back[a] * slope2[rows, :]
        grad = grad.astype(BF16)
        g2_ref[rows, :] = grad
        g2p[a, 16 : 16 + HEIGHT, :] = grad

    back = spread_conv(g2p, w_ref, 1, 16, 1, True)
    for a in range(GROUPS):
        rows = slice(HEIGHT * a, HEIGHT * (a + 1))
        grad = g2_ref[rows, :].astype(F32) + back[a] * slope1[rows, :]
        g1_ref[rows, :] = grad.astype(BF16)


def final_kernel(a2_ref, s2_ref, g1_ref, w_ref, send_ref, a2p):
    clear_edges(a2p, 32)
    for a in range(GROUPS):
        a2p[a, 32 : 32 + HEIGHT, :] = a2_ref[HEIGHT * a : HEIGHT * (a + 1), :]
    branch = spread_conv(a2p, w_ref, 2, 32, 2, False)
    state, grads = [], []
    for a in range(GROUPS):
        rows = slice(HEIGHT * a, HEIGHT * (a + 1))
        state.append(s2_ref[rows, :].astype(F32) + branch[a])
        grads.append(g1_ref[rows, :].astype(F32))

    blocks = grads + state
    for k in range(6):
        send_ref[:, 16 * k : 16 * k + 16, :] = blocks[k][:, 0:128].astype(BF16).reshape(16, 16, 128)
    for k in range(3):
        both = jnp.concatenate([blocks[2 * k][:, 128:192], blocks[2 * k + 1][:, 128:192]], axis=1)
        send_ref[:, 96 + 16 * k : 112 + 16 * k, :] = both.astype(BF16).reshape(16, 16, 128)
    third = jnp.concatenate([grads[2][:, 128:192], jnp.zeros((HEIGHT, 64), F32)], axis=1)
    first = jnp.concatenate([grads[0][:, 128:192], grads[1][:, 128:192]], axis=1)
    parts = [grads[0][:, 0:128], grads[1][:, 0:128], grads[2][:, 0:128], first, third]
    index = lax.broadcasted_iota(jnp.int32, (HEIGHT, 128), 0)
    inner = index % 16
    halo = jnp.zeros((HEIGHT, 128), F32)
    for n, part in enumerate(parts):
        p = 2 * n
        above = pltpu.roll(part, p + 1, 0)
        halo = jnp.where((inner == p) & (index >= 16), above, halo)
        p = 2 * n + 1
        below = pltpu.roll(part, (HEIGHT + p - 16) % HEIGHT, 0)
        halo = jnp.where((inner == p) & (index < HEIGHT - 16), below, halo)
    send_ref[:, 144:160, :] = halo.astype(BF16).reshape(16, 16, 128)


def wgrad_kernel(a0_ref, a1_ref, a2_ref, g1_ref, g2_ref, g3_ref, order_ref, keep_ref, give_ref, gp, acts):
    order = order_ref[...]

    def store(tap, value):
        keep_ref[tap] = value[0:96, :].astype(BF16)
        give_ref[tap] = value[96:192, :].astype(BF16)

    def spread_grad(layer, act_ref, grad_ref, width, step):
        for a in range(GROUPS):
            gp[a, 0:width, :] = jnp.zeros((width, CH), BF16)
            gp[a, width : width + HEIGHT, :] = grad_ref[HEIGHT * a : HEIGHT * (a + 1), :]
            gp[a, width + HEIGHT : 2 * width + HEIGHT, :] = jnp.zeros((width, CH), BF16)
        acts[...] = dot_t(order, act_ref[...]).astype(BF16)
        for j in range(3):
            off = (1 - j) * step
            sources = [a for a in range(GROUPS) if 0 <= a + off < GROUPS]
            lo, n = sources[0], len(sources)
            left = acts[:, HEIGHT * lo : HEIGHT * (lo + n)]
            for i in range(3):
                at = width * (2 - i)
                right = gp[lo + off : lo + off + n, at : at + HEIGHT, :].reshape(n * HEIGHT, CH)
                store(9 * layer + 3 * i + j, dot(left, right))

    spread_grad(2, a2_ref, g3_ref, 32, 2)
    spread_grad(1, a1_ref, g2_ref, 16, 1)
    shifted = [[], g1_ref[...], []]
    for a in range(GROUPS):
        rows = g1_ref[HEIGHT * a : HEIGHT * (a + 1), :].astype(F32)
        shifted[0].append(shifted_rows(rows, 1).astype(BF16))
        shifted[2].append(shifted_rows(rows, -1).astype(BF16))
    shifted[0] = jnp.concatenate(shifted[0], axis=0)
    shifted[2] = jnp.concatenate(shifted[2], axis=0)
    for j in range(3):
        acts[...] = dot_t(order, a0_ref[j]).astype(BF16)
        for i in range(3):
            store(3 * i + j, dot(acts[...], shifted[i]))


PIECES = (
    ((0, 0, 72),),
    ((0, 72, 144),),
    ((0, 144, 192), (1, 0, 24)),
    ((1, 24, 96),),
    ((1, 96, 168),),
    ((1, 168, 192), (2, 0, 48)),
    ((2, 48, 120),),
    ((2, 120, 192),),
)


def split_kernel(keep_ref, got_ref, part_ref, send_ref):
    send_ref[:, 256:416, :] = part_ref[...]
    total = (keep_ref[...].astype(F32) + got_ref[...].astype(F32)).astype(BF16)
    for h in range(2):
        for t, pieces in enumerate(PIECES):
            for group in range(4):
                parts = []
                for tap in range(7 * group, min(7 * group + 7, 27)):
                    for j, lo, hi in pieces:
                        at = 48 * h + 16 * j
                        parts.append(total[tap, at : at + 16, lo:hi])
                parts.append(jnp.zeros((16, 80 if group == 3 else 8), BF16))
                line = jnp.concatenate(parts, axis=1)
                for n in range(4):
                    at = 64 * group + 16 * n
                    send_ref[8 * h + t, at : at + 16, :] = line[:, 128 * n : 128 * n + 128]


def gather_kernel(got_ref, send_ref, total_ref):
    total = got_ref[0, 0:256, :].astype(F32)
    for s in range(1, 16):
        total = total + got_ref[s, 0:256, :].astype(F32)
    total_ref[...] = total
    for z in range(16):
        send_ref[z] = total_ref[pl.ds(z, 16, stride=16), :].astype(BF16)


def finish_kernel(scale, got_ref, out_ref):
    total = got_ref[0].astype(F32)
    for z in range(1, 16):
        total = total + got_ref[z].astype(F32)
    total = total * scale
    for tap in range(27):
        start = 512 * (tap // 7) + 72 * (tap % 7)
        parts = []
        while sum(part.shape[1] for part in parts) < 72:
            at = start + sum(part.shape[1] for part in parts)
            end = min(start + 72, (at // 128 + 1) * 128)
            row = at // 128
            parts.append(total[row : row + 1, at % 128 : at % 128 + end - at])
        out_ref[tap : tap + 1, :] = parts[0] if len(parts) == 1 else jnp.concatenate(parts, axis=1)


def last_kernel(recv_ref, x_ref, w_ref, out_ref, grad_ref, padded, slope_ref, grads_ref):
    def tile(k):
        at = 256 + 16 * k
        return recv_ref[:, at : at + 16, :].reshape(HEIGHT, 128).astype(F32)

    lows = [tile(k) for k in range(6)]
    highs = []
    for k in range(3):
        both = tile(6 + k)
        highs += [both[:, 0:64], both[:, 64:128]]
    halo = tile(9)
    inner = lax.broadcasted_iota(jnp.int32, (HEIGHT, CH), 0) % 16

    def pair(left, right):
        return jnp.concatenate([left, right], axis=1)

    final = [jnp.concatenate([lows[3 + a], highs[3 + a]], axis=1) for a in range(GROUPS)]
    for p in range(WIDTH // 2):
        a, b = (2 * p) // 16, (2 * p) % 16
        left = final[a][16 * b : 16 * b + 16]
        right = final[a][16 * b + 16 : 16 * b + 32]
        out_ref[0, :, 384 * p : 384 * p + 384] = pair(left, right).astype(BF16)

    zeros = jnp.zeros((16, CH), BF16)
    for i in range(3):
        padded[i, 0:16, :] = zeros
        padded[i, 16 + CELLS : 32 + CELLS, :] = zeros
    for a in range(GROUPS):
        at = 16 + HEIGHT * a
        here = jnp.concatenate([lows[a], highs[a]], axis=1)
        grads_ref[HEIGHT * a : HEIGHT * (a + 1), :] = here

        def edge(row, p_lo, p_hi, lane):
            low = pltpu.roll(halo, (row - p_lo) % HEIGHT, 0)
            high = pltpu.roll(halo, (row - p_hi) % HEIGHT, 0)[:, lane : lane + 64]
            return jnp.concatenate([low, high], axis=1)

        hi_slot, lane = ((6, 0), (6, 64), (8, 0))[a]
        above = edge(0, 2 * a, hi_slot, lane)
        below = edge(15, 2 * a + 1, hi_slot + 1, lane)
        after = jnp.where(inner == 15, below, pltpu.roll(here, HEIGHT - 1, 0))
        before = jnp.where(inner == 0, above, pltpu.roll(here, 1, 0))
        padded[0, at : at + HEIGHT, :] = after.astype(BF16)
        padded[1, at : at + HEIGHT, :] = here.astype(BF16)
        padded[2, at : at + HEIGHT, :] = before.astype(BF16)

    for p in range(WIDTH // 2):
        values = x_ref[0, :, 384 * p : 384 * p + 384].astype(F32)
        slope = gelu_and_slope(values)[1]
        slope_ref[32 * p : 32 * p + 16, :] = slope[:, 0:192]
        slope_ref[32 * p + 16 : 32 * p + 32, :] = slope[:, 192:384]

    total = None
    for i in range(3):
        for j in range(3):
            at = 16 * (2 - j)
            term = dot_t(padded[i, at : at + CELLS, :], w_ref[3 * i + j])
            total = term if total is None else total + term
    result = grads_ref[...] + total * slope_ref[...]
    for p in range(WIDTH // 2):
        left = result[32 * p : 32 * p + 16]
        right = result[32 * p + 16 : 32 * p + 32]
        grad_ref[0, :, 384 * p : 384 * p + 384] = pair(left, right).astype(BF16)


def body(inputs, cotangent, weights):
    count = math.prod(lax.axis_size(axis) for axis in DP + SPACE)
    scale = 1.0 / math.sqrt(count * ROWS * WIDTH)
    core = lax.axis_index("core")

    place = jnp.arange(CH)
    half = (core + place // 96) % 2
    channel = 12 * (place % 16) + 6 * half + 3 * ((place // 48) % 2) + (place // 16) % 3
    order = (channel[:, None] == jnp.arange(CH)[None, :]).astype(BF16)

    send = call(
        pack_kernel,
        shape(16, 288, 128),
        after=(inputs, cotangent),
        scratch=(
            pltpu.VMEM((1, ROWS, 9216), BF16),
            pltpu.VMEM((1, ROWS, 9216), BF16),
            pltpu.VMEM((ROWS, 9216), BF16),
            pltpu.SemaphoreType.DMA((2,)),
        ),
        moved=2500000,
    )
    recv = lax.all_to_all(send, SPACE, 0, 0, tiled=True)
    kernels = weights.reshape(27, CH, CH)
    a0, a1, a2, g1, g2, g3, s2 = call(
        main_kernel,
        (shape(3, CELLS, CH),) + (shape(CELLS, CH),) * 6,
        recv,
        kernels,
        scratch=(
            pltpu.VMEM((GROUPS, HEIGHT + 32, CH), BF16),
            pltpu.VMEM((GROUPS, HEIGHT + 32, CH), BF16),
            pltpu.VMEM((GROUPS, HEIGHT + 64, CH), BF16),
            pltpu.VMEM((CELLS, CH), F32),
            pltpu.VMEM((CELLS, CH), F32),
        ),
        flops=4 * 2 * CELLS * 9 * CH * CH,
        moved=9000000,
    )
    keep, give = call(
        wgrad_kernel,
        (shape(27, 96, CH), shape(27, 96, CH)),
        a0, a1, a2, g1, g2, g3, order,
        scratch=(pltpu.VMEM((GROUPS, HEIGHT + 64, CH), BF16), pltpu.VMEM((CH, CELLS), BF16)),
        flops=3 * 2 * CELLS * 9 * CH * CH,
        moved=7000000,
    )
    got = lax.ppermute(give, "core", [(0, 1), (1, 0)])
    part = call(
        final_kernel,
        shape(16, 160, 128),
        a2, s2, g1, kernels,
        scratch=(pltpu.VMEM((GROUPS, HEIGHT + 64, CH), BF16),),
        flops=2 * CELLS * 9 * CH * CH,
        moved=4500000,
    )
    send = call(split_kernel, shape(16, 416, 128), keep, got, part, moved=5000000)
    back = lax.all_to_all(send, SPACE, 0, 0, tiled=True)
    send, _ = call(
        gather_kernel, (shape(16, 16, 128), shape(256, 128, dtype=F32)), back, moved=2000000
    )
    got = lax.all_to_all(send, "z", 0, 0, tiled=True)
    weight_grad = call(
        lambda *refs: finish_kernel(scale, *refs), shape(27, 72, dtype=F32), got, moved=150000
    )
    outputs, input_grad = call(
        last_kernel,
        (shape(1, ROWS, 9216), shape(1, ROWS, 9216)),
        back, inputs, kernels,
        scratch=(
            pltpu.VMEM((3, CELLS + 32, CH), BF16),
            pltpu.VMEM((CELLS, CH), F32),
            pltpu.VMEM((CELLS, CH), F32),
        ),
        flops=2 * CELLS * 9 * CH * CH,
        moved=3000000,
    )
    return outputs, input_grad, weight_grad


def solution(mesh):
    devices = mesh.devices.reshape(16, 2, 4, 4)
    wide = Mesh(devices, DP + SPACE)
    placed = (P(DP, SPACE, None), P(DP, SPACE, None), P())
    return jax.shard_map(
        body,
        mesh=wide,
        in_specs=placed,
        out_specs=(P(DP, SPACE, None), P(DP, SPACE, None), P(None, DP + SPACE)),
        check_vma=False,
    )
```

time: 722 us -> 104 us (0.14)
  the two profiles are of different devices: /device:TPU:2 before, /device:TPU:8 now
where the time goes in v1:
time: 104 us; the launch traced here: 103 us
  starting transfers between devices  27.5 us (26%)
  blocking collectives  27.1 us (26%)
  waiting for transfers between devices  18.6 us (18%)
  Pallas kernels  16.5 us (16%)
  local copies, waits for them, and re-layouts  12.5 us (12%)
    all_to_all x1, blocking collectives, body(): back = lax.all_to_all(send, SPACE, 0, 0, tiled=True)  27.1 us
    pallas_call x8, Pallas kernels, call(): pl.pallas_call(kernel, out_shape=out_shape, in_specs=[pl.BlockSpec(memory...  16.5 us
    all_to_all x1, starting transfers between devices, body(): got = lax.all_to_all(send, 'z', 0, 0, tiled=True)  15.6 us
    all_to_all x1, starting transfers between devices, body(): recv = lax.all_to_all(send, SPACE, 0, 0, tiled=True)  9.96 us
    all_to_all x1, waiting for transfers between devices, body(): got = lax.all_to_all(send, 'z', 0, 0, tiled=True)  9.14 us
    unnamed x13, local copies, waits for them, and re-layouts  7.85 us
    all_to_all x1, waiting for transfers between devices, body(): recv = lax.all_to_all(send, SPACE, 0, 0, tiled=True)  7.22 us
    reshape x1, local copies, waits for them, and re-layouts, body(): kernels = weights.reshape(27, CH, CH)  4.65 us
  transfers between devices with their start and end apart: 3, of which 3 were waited for; matrix products, arithmetic and copies ran while one was open for 8% of the time, Pallas kernels for 3%

profile of v1, /device:TPU:8, one launch (start us, length us, event | category | flops | bytes accessed | tf_op | source)
XLA Modules:
  0.0 103.0 jit_solution(6016800310481807777)
XLA Ops:
  0.6 0.0 copy-start.2
  0.6 1.0 copy-done.2
  1.6 0.0 copy-start.4
  1.6 1.0 copy-done.4
  2.6 0.0 copy-start.5
  2.6 1.7 %shard_map.58 = bf16[16,288,128]{2,1,0:T(8,128)(2,1)} custom-call(bf16[1,16,9216]{2,1,0:T(8,128)(2,1)S(1)} %copy-done.2, bf16[1,16,9216]{2,1,0:T(8,128)(2,1)S(1)} %copy-done.4), custom_call_target="tpu_custom_call" | custom-call | bytes 2500000 | tf_op jit(solution)/shard_map/pallas_call | solution.py:48
  4.3 10.0 %all-to-all-start = ((bf16[16,288,128]{2,1,0:T(8,128)(2,1)}), bf16[16,288,128]{2,1,0:T(8,128)(2,1)}, u32[]{:S(2)}, u32[]{:S(2)}) async-start(bf16[16,288,128]{2,1,0:T(8,128)(2,1)} %shard_map.58), calls=%async_computation | async-start | bytes 2359296 | tf_op jit(solution)/shard_map/all_to_all | solution.py:418
  14.2 0.0 copy-done.5
  14.2 3.3 %copy.7 = bf16[3,9,36864]{2,1,0:T(8,128)(2,1)} copy(bf16[3,9,36864]{2,0,1:T(4,128)(2,1)S(1)} %copy-done.5) | data formatting | bytes 3981312 | tf_op args[2]
  17.5 4.6 %reshape.80.w_ref = bf16[27,192,192]{2,1,0:T(8,128)(2,1)S(1)} reshape(bf16[3,9,36864]{2,1,0:T(8,128)(2,1)} %copy.7) | data formatting | bytes 3981312 | tf_op jit(solution)/shard_map/reshape | solution.py:419
  22.2 0.1 fusion.order_ref
  22.3 7.2 %all-to-all-done.recv_ref = bf16[16,288,128]{2,1,0:T(8,128)(2,1)} async-done(((bf16[16,288,128]{2,1,0:T(8,128)(2,1)}), bf16[16,288,128]{2,1,0:T(8,128)(2,1)}, u32[]{:S(2)}, u32[]{:S(2)}) %all-to-all-start) | async-done | bytes 1179680 | tf_op jit(solution)/shard_map/all_to_all | solution.py:418
  29.5 6.8 %shard_map.59 = (bf16[3,768,192]{2,1,0:T(8,128)(2,1)S(1)}, bf16[768,192]{1,0:T(8,128)(2,1)S(1)}, bf16[768,192]{1,0:T(8,128)(2,1)S(1)}, bf16[768,192]{1,0:T(8,128...) custom-call(bf16[16,288,128]{2,1,0:T(8,128)(2,1)} %all-to-all-done.recv_ref, ...), custom_call_target="tpu_custom_call" | custom-call | flops 2038431744 | bytes 9000000 | tf_op jit(solution)/shard_map/pallas_call | solution.py:48
  36.4 2.5 %shard_map.60 = (bf16[27,96,192]{2,1,0:T(8,128)(2,1)S(1)}, bf16[27,96,192]{2,1,0:T(8,128)(2,1)S(1)}) custom-call(bf16[3,768,192]{2,1,0:T(8,128)(2,1)S(1)} %get-tuple-element.15.a0_ref, bf16[768,192]{1,0:T(8,128)(2,1)S(1)} %get-tuple-element.16.a1_ref, bf16[768,192]{1,0:T(8,128)(2,1)S(1)} %get-tuple-element.17.a2_ref, ...), custom_call_target="tpu_custom_call" | custom-call | flops 1528823808 | bytes 7000000 | tf_op jit(solution)/shard_map/pallas_call | solution.py:48
  38.9 1.9 %collective-permute-start = (bf16[27,96,192]{2,1,0:T(8,128)(2,1)S(1)}, bf16[27,96,192]{2,1,0:T(8,128)(2,1)S(1)}, u32[]{:S(2)}, u32[]{:S(2)}) collective-permute-start(bf16[27,96,192]{2,1,0:T(8,128)(2,1)S(1)} %get-tuple-element.22), channel_id=1, source_target_pairs={{0,16},{16,0},{1,17},{17,1},{2,18},{18,2},{3,19},{19,3},{4,20},{20... | collective-permute-start | bytes 2985992 | tf_op jit(solution)/shard_map/ppermute | solution.py:443
  40.8 0.8 shard_map.61.part_ref
  41.6 2.2 %collective-permute-done.got_ref = bf16[27,96,192]{2,1,0:T(8,128)(2,1)S(1)} collective-permute-done((bf16[27,96,192]{2,1,0:T(8,128)(2,1)S(1)}, bf16[27,96,192]{2,1,0:T(8,128)(2,1)S(1)}, u32[]{:S(2)}, u32[]{:S(2)}) %collective-permute-start) | collective-permute-done | bytes 995360 | tf_op jit(solution)/shard_map/ppermute | solution.py:443
  43.9 0.8 shard_map.62
  44.6 27.1 %all_to_all.15.recv_ref.got_ref = bf16[16,416,128]{2,1,0:T(8,128)(2,1)S(1)} all-to-all(bf16[16,416,128]{2,1,0:T(8,128)(2,1)S(1)} %shard_map.62), channel_id=1, replica_groups=mesh['z'=16,'core'=2,'x'=4,'y'=4] {'x','y'}, dimensions={0} | all-to-all | bytes 3407872 | tf_op jit(solution)/shard_map/all_to_all | solution.py:453
  71.7 0.0 copy-start.3
  71.7 0.8 shard_map.64
  72.6 0.0 copy-start
  72.6 1.2 %copy-done = bf16[16,416,128]{2,1,0:T(8,128)(2,1)} copy-done((bf16[16,416,128]{2,1,0:T(8,128)(2,1)}, bf16[16,416,128]{2,1,0:T(8,128)(2,1)S(1)}, u32[]{:S(2)}) %copy-start) | copy-done | bytes 1703960
  73.8 15.6 %all-to-all-start.2 = ((bf16[16,16,128]{2,1,0:T(8,128)(2,1)}), bf16[16,16,128]{2,1,0:T(8,128)(2,1)S(1)}, u32[]{:S(2)}, u32[]{:S(2)}) async-start(bf16[16,16,128]{2,1,0:T(8,128)(2,1)} %get-tuple-element.26), calls=%async_computation.2 | async-start | bytes 131072 | tf_op jit(solution)/shard_map/all_to_all | solution.py:457
  89.4 0.0 copy-done.3
  89.4 0.0 copy-start.1
  89.4 1.4 %copy-done.1 = bf16[16,416,128]{2,1,0:T(8,128)(2,1)S(1)} copy-done((bf16[16,416,128]{2,1,0:T(8,128)(2,1)S(1)}, bf16[16,416,128]{2,1,0:T(8,128)(2,1)}, u32[]{:S(2)}) %copy-start.1) | copy-done | bytes 1703960
  90.9 2.2 %shard_map.63 = (bf16[1,16,9216]{2,1,0:T(8,128)(2,1)}, bf16[1,16,9216]{2,1,0:T(8,128)(2,1)}) custom-call(bf16[16,416,128]{2,1,0:T(8,128)(2,1)S(1)} %copy-done.1, bf16[1,16,9216]{2,1,0:T(8,128)(2,1)S(1)} %copy-done.3, bf16[27,192,192]{2,1,0:T(8,128)(2,1)S(1)} %reshape.80.w_ref), custom_call_target="tpu_custom_call" | custom-call | flops 509607936 | bytes 3000000 | tf_op jit(solution)/shard_map/pallas_call | solution.py:48
  93.1 9.1 %all-to-all-done.2.refs_0_ = bf16[16,16,128]{2,1,0:T(8,128)(2,1)S(1)} async-done(((bf16[16,16,128]{2,1,0:T(8,128)(2,1)}), bf16[16,16,128]{2,1,0:T(8,128)(2,1)S(1)}, u32[]{:S(2)}, u32[]{:S(2)}) %all-to-all-start.2) | async-done | bytes 65568 | tf_op jit(solution)/shard_map/all_to_all | solution.py:457
  102.3 0.7 shard_map.65
  (1 shorter events, 0.0 us)
Async XLA Ops:
  0.6 1.0 copy-start.2
  1.6 1.0 copy-start.4
  2.6 11.7 %copy-start.5 = (bf16[3,9,36864]{2,0,1:T(4,128)(2,1)S(1)}, bf16[3,9,36864]{2,0,1:T(4,128)(2,1)}, u32[]{:S(2)}) copy-start(bf16[3,9,36864]{2,0,1:T(4,128)(2,1)} %param.5) | copy-start | bytes 5971972
  4.3 25.2 %all-to-all-start = ((bf16[16,288,128]{2,1,0:T(8,128)(2,1)}), bf16[16,288,128]{2,1,0:T(8,128)(2,1)}, u32[]{:S(2)}, u32[]{:S(2)}) async-start(bf16[16,288,128]{2,1,0:T(8,128)(2,1)} %shard_map.58), calls=%async_computation | async-start | bytes 2359296 | tf_op jit(solution)/shard_map/all_to_all | solution.py:418
  38.9 5.0 %collective-permute-start = (bf16[27,96,192]{2,1,0:T(8,128)(2,1)S(1)}, bf16[27,96,192]{2,1,0:T(8,128)(2,1)S(1)}, u32[]{:S(2)}, u32[]{:S(2)}) collective-permute-start(bf16[27,96,192]{2,1,0:T(8,128)(2,1)S(1)} %get-tuple-element.22), channel_id=1, source_target_pairs={{0,16},{16,0},{1,17},{17,1},{2,18},{18,2},{3,19},{19,3},{4,20},{20... | collective-permute-start | bytes 2985992 | tf_op jit(solution)/shard_map/ppermute | solution.py:443
  71.7 17.7 %copy-start.3 = (bf16[1,16,9216]{2,1,0:T(8,128)(2,1)S(1)}, bf16[1,16,9216]{2,1,0:T(8,128)(2,1)}, u32[]{:S(2)}) copy-start(bf16[1,16,9216]{2,1,0:T(8,128)(2,1)} %x_ref.1) | copy-start | bytes 884740
  72.6 1.2 %copy-start = (bf16[16,416,128]{2,1,0:T(8,128)(2,1)}, bf16[16,416,128]{2,1,0:T(8,128)(2,1)S(1)}, u32[]{:S(2)}) copy-start(bf16[16,416,128]{2,1,0:T(8,128)(2,1)S(1)} %all_to_all.15.recv_ref.got_ref) | copy-start | bytes 5111812
  73.8 28.5 %all-to-all-start.2 = ((bf16[16,16,128]{2,1,0:T(8,128)(2,1)}), bf16[16,16,128]{2,1,0:T(8,128)(2,1)S(1)}, u32[]{:S(2)}, u32[]{:S(2)}) async-start(bf16[16,16,128]{2,1,0:T(8,128)(2,1)} %get-tuple-element.26), calls=%async_computation.2 | async-start | bytes 131072 | tf_op jit(solution)/shard_map/all_to_all | solution.py:457
  89.4 1.5 %copy-start.1 = (bf16[16,416,128]{2,1,0:T(8,128)(2,1)S(1)}, bf16[16,416,128]{2,1,0:T(8,128)(2,1)}, u32[]{:S(2)}) copy-start(bf16[16,416,128]{2,1,0:T(8,128)(2,1)} %copy-done) | copy-start | bytes 5111812

commit v2 on v1

--- a/solution.py
+++ b/solution.py
@@ -22,6 +22,7 @@
 GELU_A = math.sqrt(2.0 / math.pi)
 GELU_B = 0.044715
 VMEM_LIMIT = 24 * 1024 * 1024
+VMEM_MOST = 60 * 1024 * 1024
 
 
 def gelu(x):
@@ -44,24 +45,27 @@
     return lax.dot_general(a, b, (((1,), (1,)), ((), ())), preferred_element_type=F32)
 
 
-def call(kernel, out_shape, *args, scratch=(), flops=0, moved=0, after=()):
+def call(kernel, out_shape, *args, scratch=(), flops=0, moved=0, remain=(), limit=VMEM_LIMIT, apart=0):
+    outputs = jax.tree.leaves(out_shape)
+    spaces = [pltpu.VMEM] * (len(outputs) - apart) + [pltpu.HBM] * apart
+    specs = [pl.BlockSpec(memory_space=space) for space in spaces]
     return pl.pallas_call(
         kernel,
         out_shape=out_shape,
-        in_specs=[pl.BlockSpec(memory_space=pltpu.VMEM)] * len(args)
-        + [pl.BlockSpec(memory_space=pl.ANY)] * len(after),
-        out_specs=jax.tree.map(lambda _: pl.BlockSpec(memory_space=pltpu.VMEM), out_shape),
+        in_specs=[pl.BlockSpec(memory_space=pltpu.HBM)] * len(remain)
+        + [pl.BlockSpec(memory_space=pltpu.VMEM)] * len(args),
+        out_specs=jax.tree.unflatten(jax.tree.structure(out_shape), specs),
         scratch_shapes=list(scratch),
-        compiler_params=pltpu.CompilerParams(vmem_limit_bytes=VMEM_LIMIT),
+        compiler_params=pltpu.CompilerParams(vmem_limit_bytes=limit),
         cost_estimate=pl.CostEstimate(flops=flops, bytes_accessed=moved, transcendentals=0),
-    )(*args, *after)
+    )(*remain, *args)
 
 
 def shape(*dims, dtype=BF16):
     return jax.ShapeDtypeStruct(dims, dtype)
 
 
-def pack_kernel(x_hbm, c_hbm, send_ref, x_ref, c_ref, act_ref, sems):
+def pack_kernel(x_hbm, c_hbm, send_hbm, x_ref, c_ref, act_ref, send_ref, sems, send_sems):
     copies = [
         pltpu.make_async_copy(x_hbm, x_ref, sems.at[0]),
         pltpu.make_async_copy(c_hbm, c_ref, sems.at[1]),
@@ -78,7 +82,7 @@
         return pair[:, base : base + 128], pair[:, base + 128 : base + 192]
 
     nothing = jnp.zeros((16, 128), BF16), jnp.zeros((16, 64), BF16)
-    act, raw, cot = [], [], []
+    act, raw, cot, leaving = [], [], [], []
     for w in range(WIDTH):
         act.append(column(lambda at: act_ref[:, at : at + 384], w))
         raw.append(column(lambda at: x_ref[0, :, at : at + 384], w))
@@ -101,6 +105,10 @@
         for k in range(6):
             both = jnp.concatenate([blocks[2 * k][1], blocks[2 * k + 1][1]], axis=1)
             send_ref[b, 192 + 16 * k : 208 + 16 * k, :] = both
+        leaving.append(pltpu.make_async_copy(send_ref.at[b], send_hbm.at[b], send_sems.at[b]))
+        leaving[b].start()
+    for copy in leaving:
+        copy.wait()
 
 
 def shifted_rows(value, by):
@@ -111,21 +119,22 @@
 
 
 def spread_conv(padded, w_ref, layer, width, step, transposed):
-    totals = [None] * GROUPS
-    for j in range(3):
-        off = (1 - j) * step if transposed else (j - 1) * step
-        outs = [a for a in range(GROUPS) if 0 <= a + off < GROUPS]
-        lo, n = outs[0], len(outs)
-        total = None
-        for i in range(3):
-            at = width * (2 - i) if transposed else width * i
-            cells = padded[lo + off : lo + off + n, at : at + HEIGHT, :].reshape(n * HEIGHT, CH)
-            kernel = w_ref[9 * layer + 3 * i + j]
-            term = dot_t(cells, kernel) if transposed else dot(cells, kernel)
-            total = term if total is None else total + term
-        for m, a in enumerate(outs):
-            part = total[m * HEIGHT : (m + 1) * HEIGHT]
-            totals[a] = part if totals[a] is None else totals[a] + part
+    totals = []
+    for a in range(GROUPS):
+        cells, taps = [], []
+        for j in range(3):
+            src = a + ((1 - j) * step if transposed else (j - 1) * step)
+            if not 0 <= src < GROUPS:
+                continue
+            for i in range(3):
+                at = width * (2 - i) if transposed else width * i
+                cells.append(padded[src, at : at + HEIGHT, :])
+                taps.append(w_ref[9 * layer + 3 * i + j])
+        cells = jnp.concatenate(cells, axis=1)
+        if transposed:
+            totals.append(dot_t(cells, jnp.concatenate(taps, axis=1)))
+        else:
+            totals.append(dot(cells, jnp.concatenate(taps, axis=0)))
     return totals
 
 
@@ -135,10 +144,31 @@
         ref[a, pad + HEIGHT : 2 * pad + HEIGHT, :] = jnp.zeros((pad, CH), BF16)
 
 
+MAIN_SCRATCH = (
+    pltpu.VMEM((16, 288, 128), BF16),
+    pltpu.VMEM((CELLS, 3 * CH), BF16),
+    pltpu.VMEM((GROUPS, HEIGHT + 32, CH), BF16),
+    pltpu.VMEM((GROUPS, HEIGHT + 32, CH), BF16),
+    pltpu.VMEM((GROUPS, HEIGHT + 64, CH), BF16),
+    pltpu.VMEM((CELLS, CH), F32),
+    pltpu.VMEM((CELLS, CH), F32),
+    pltpu.SemaphoreType.DMA((3,)),
+)
+
+
 def main_kernel(
-    recv_ref, w_ref, a0_ref, a1_ref, a2_ref, g1_ref, g2_ref, g3_ref, s2_ref,
-    a1p, g2p, g3p, slope1, slope2,
+    recv_hbm, w_ref, a0_ref, a1_ref, a2_ref, g1_ref, g2_ref, g3_ref, s2_ref,
+    recv_ref, a0p, a1p, g2p, g3p, slope1, slope2, sems,
 ):
+    def rows_copy(n, lo, hi):
+        part = pltpu.make_async_copy(
+            recv_hbm.at[:, lo:hi, :], recv_ref.at[:, lo:hi, :], sems.at[n]
+        )
+        part.start()
+        return part
+
+    moving = [rows_copy(0, 0, 144), rows_copy(1, 192, 288), rows_copy(2, 144, 192)]
+
     def block(k):
         lo = recv_ref[:, 16 * k : 16 * k + 16, :].reshape(HEIGHT, 128)
         at = 192 + 16 * (k // 2)
@@ -148,28 +178,33 @@
     for ref, pad in ((a1p, 16), (g2p, 16), (g3p, 32)):
         clear_edges(ref, pad)
 
+    moving[0].wait()
+    moving[1].wait()
     state = []
     for a in range(GROUPS):
         rows = slice(HEIGHT * a, HEIGHT * (a + 1))
-        a0_ref[0, rows, :] = block(a)
         raw = block(3 + a)
         state.append(raw)
-        a0_ref[1, rows, :] = gelu(raw.astype(F32)).astype(BF16)
-        a0_ref[2, rows, :] = block(6 + a)
+        for j in range(3):
+            value = gelu(raw.astype(F32)).astype(BF16) if j == 1 else block(3 * j + a)
+            a0_ref[j, rows, :] = value
+            a0p[rows, CH * j : CH * (j + 1)] = value
+
+    sums = [[], [], []]
+    for a in range(GROUPS):
+        rows = slice(HEIGHT * a, HEIGHT * (a + 1))
+        for i in range(3):
+            taps = jnp.concatenate([w_ref[3 * i + j] for j in range(3)], axis=0)
+            sums[i].append(dot(a0p[rows, :], taps))
+    moving[2].wait()
+    for a in range(GROUPS):
         cot = block(9 + a)
-        g3_ref[rows, :] = cot
+        g3_ref[HEIGHT * a : HEIGHT * (a + 1), :] = cot
         g3p[a, 32 : 32 + HEIGHT, :] = cot
-
-    sums = []
-    for i in range(3):
-        total = None
-        for j in range(3):
-            term = dot(a0_ref[j], w_ref[3 * i + j])
-            total = term if total is None else total + term
-        sums.append(total)
-    for a in range(GROUPS):
-        rows = slice(HEIGHT * a, HEIGHT * (a + 1))
-        branch = shifted_rows(sums[0][rows], -1) + sums[1][rows] + shifted_rows(sums[2][rows], 1)
+    back = spread_conv(g3p, w_ref, 2, 32, 2, True)
+    for a in range(GROUPS):
+        rows = slice(HEIGHT * a, HEIGHT * (a + 1))
+        branch = shifted_rows(sums[0][a], -1) + sums[1][a] + shifted_rows(sums[2][a], 1)
         state[a] = (state[a].astype(F32) + branch).astype(BF16)
         act, slope = gelu_and_slope(state[a].astype(F32))
         act = act.astype(BF16)
@@ -187,7 +222,6 @@
         a2_ref[rows, :] = act
         s2_ref[rows, :] = state[a]
 
-    back = spread_conv(g3p, w_ref, 2, 32, 2, True)
     for a in range(GROUPS):
         rows = slice(HEIGHT * a, HEIGHT * (a + 1))
         grad = g3_ref[rows, :].astype(F32) + back[a] * slope2[rows, :]
@@ -303,13 +337,16 @@
                     send_ref[8 * h + t, at : at + 16, :] = line[:, 128 * n : 128 * n + 128]
 
 
-def gather_kernel(got_ref, send_ref, total_ref):
+def gather_kernel(got_ref, send_ref, rest_hbm, total_ref, sem):
+    rest = pltpu.make_async_copy(got_ref.at[:, 256:416, :], rest_hbm, sem)
+    rest.start()
     total = got_ref[0, 0:256, :].astype(F32)
     for s in range(1, 16):
         total = total + got_ref[s, 0:256, :].astype(F32)
     total_ref[...] = total
     for z in range(16):
         send_ref[z] = total_ref[pl.ds(z, 16, stride=16), :].astype(BF16)
+    rest.wait()
 
 
 def finish_kernel(scale, got_ref, out_ref):
@@ -330,8 +367,7 @@
 
 def last_kernel(recv_ref, x_ref, w_ref, out_ref, grad_ref, padded, slope_ref, grads_ref):
     def tile(k):
-        at = 256 + 16 * k
-        return recv_ref[:, at : at + 16, :].reshape(HEIGHT, 128).astype(F32)
+        return recv_ref[:, 16 * k : 16 * k + 16, :].reshape(HEIGHT, 128).astype(F32)
 
     lows = [tile(k) for k in range(6)]
     highs = []
@@ -380,12 +416,13 @@
         slope_ref[32 * p : 32 * p + 16, :] = slope[:, 0:192]
         slope_ref[32 * p + 16 : 32 * p + 32, :] = slope[:, 192:384]
 
-    total = None
+    cells, taps = [], []
     for i in range(3):
         for j in range(3):
             at = 16 * (2 - j)
-            term = dot_t(padded[i, at : at + CELLS, :], w_ref[3 * i + j])
-            total = term if total is None else total + term
+            cells.append(padded[i, at : at + CELLS, :])
+            taps.append(w_ref[3 * i + j])
+    total = dot_t(jnp.concatenate(cells, axis=1), jnp.concatenate(taps, axis=1))
     result = grads_ref[...] + total * slope_ref[...]
     for p in range(WIDTH // 2):
         left = result[32 * p : 32 * p + 16]
@@ -406,29 +443,27 @@
     send = call(
         pack_kernel,
         shape(16, 288, 128),
-        after=(inputs, cotangent),
+        remain=(inputs, cotangent),
         scratch=(
             pltpu.VMEM((1, ROWS, 9216), BF16),
             pltpu.VMEM((1, ROWS, 9216), BF16),
             pltpu.VMEM((ROWS, 9216), BF16),
+            pltpu.VMEM((16, 288, 128), BF16),
             pltpu.SemaphoreType.DMA((2,)),
+            pltpu.SemaphoreType.DMA((16,)),
         ),
         moved=2500000,
+        apart=1,
+        limit=VMEM_MOST,
     )
     recv = lax.all_to_all(send, SPACE, 0, 0, tiled=True)
     kernels = weights.reshape(27, CH, CH)
     a0, a1, a2, g1, g2, g3, s2 = call(
         main_kernel,
         (shape(3, CELLS, CH),) + (shape(CELLS, CH),) * 6,
-        recv,
         kernels,
-        scratch=(
-            pltpu.VMEM((GROUPS, HEIGHT + 32, CH), BF16),
-            pltpu.VMEM((GROUPS, HEIGHT + 32, CH), BF16),
-            pltpu.VMEM((GROUPS, HEIGHT + 64, CH), BF16),
-            pltpu.VMEM((CELLS, CH), F32),
-            pltpu.VMEM((CELLS, CH), F32),
-        ),
+        remain=(recv,),
+        scratch=MAIN_SCRATCH,
         flops=4 * 2 * CELLS * 9 * CH * CH,
         moved=9000000,
     )
@@ -451,8 +486,13 @@
     )
     send = call(split_kernel, shape(16, 416, 128), keep, got, part, moved=5000000)
     back = lax.all_to_all(send, SPACE, 0, 0, tiled=True)
-    send, _ = call(
-        gather_kernel, (shape(16, 16, 128), shape(256, 128, dtype=F32)), back, moved=2000000
+    send, rest = call(
+        gather_kernel,
+        (shape(16, 16, 128), shape(16, 160, 128)),
+        back,
+        scratch=(pltpu.VMEM((256, 128), F32), pltpu.SemaphoreType.DMA),
+        moved=2500000,
+        apart=1,
     )
     got = lax.all_to_all(send, "z", 0, 0, tiled=True)
     weight_grad = call(
@@ -461,7 +501,7 @@
     outputs, input_grad = call(
         last_kernel,
         (shape(1, ROWS, 9216), shape(1, ROWS, 9216)),
-        back, inputs, kernels,
+        rest, inputs, kernels,
         scratch=(
             pltpu.VMEM((3, CELLS + 32, CH), BF16),
             pltpu.VMEM((CELLS, CH), F32),

time: 104 us -> 101 us (0.971)
  local copies, waits for them, and re-layouts: 12.5 us -> 9.84 us
    unnamed x13 -> x9, local copies, waits for them, and re-layouts: 7.85 us -> 5.19 us
where the time goes in v2:
time: 101 us; the launch traced here: 100 us
  starting transfers between devices  27.5 us (27%)
  blocking collectives  27.1 us (27%)
  waiting for transfers between devices  19.1 us (19%)
  Pallas kernels  15.8 us (16%)
  local copies, waits for them, and re-layouts  9.84 us (10%)
    all_to_all x1, blocking collectives, body(): back = lax.all_to_all(send, SPACE, 0, 0, tiled=True)  27.1 us
    pallas_call x8, Pallas kernels, call(): pl.pallas_call(kernel, out_shape=out_shape, in_specs=[pl.BlockSpec(memory...  15.8 us
    all_to_all x1, starting transfers between devices, body(): got = lax.all_to_all(send, 'z', 0, 0, tiled=True)  15.6 us
    all_to_all x1, starting transfers between devices, body(): recv = lax.all_to_all(send, SPACE, 0, 0, tiled=True)  9.95 us
    all_to_all x1, waiting for transfers between devices, body(): got = lax.all_to_all(send, 'z', 0, 0, tiled=True)  9.64 us
    all_to_all x1, waiting for transfers between devices, body(): recv = lax.all_to_all(send, SPACE, 0, 0, tiled=True)  7.22 us
    unnamed x9, local copies, waits for them, and re-layouts  5.19 us
    reshape x1, local copies, waits for them, and re-layouts, body(): kernels = weights.reshape(27, CH, CH)  4.65 us
  transfers between devices with their start and end apart: 3, of which 3 were waited for; matrix products, arithmetic and copies ran while one was open for 8% of the time, Pallas kernels for 3%

profile of v2, /device:TPU:8, one launch (start us, length us, event | category | flops | bytes accessed | tf_op | source)
XLA Modules:
  0.0 100.2 jit_solution(2345366636056219396)
XLA Ops:
  0.6 0.0 copy-start.3
  0.6 2.6 %shard_map.58 = bf16[16,288,128]{2,1,0:T(8,128)(2,1)} custom-call(bf16[1,16,9216]{2,1,0:T(8,128)(2,1)} %x_ref.1, bf16[1,16,9216]{2,1,0:T(8,128)(2,1)} %c_hbm.1), custom_call_target="tpu_custom_call" | custom-call | bytes 2500000 | tf_op jit(solution)/shard_map/pallas_call | solution.py:52
  3.2 10.0 %all-to-all-start = ((bf16[16,288,128]{2,1,0:T(8,128)(2,1)}), bf16[16,288,128]{2,1,0:T(8,128)(2,1)}, u32[]{:S(2)}, u32[]{:S(2)}) async-start(bf16[16,288,128]{2,1,0:T(8,128)(2,1)} %shard_map.58), calls=%async_computation | async-start | bytes 2359296 | tf_op jit(solution)/shard_map/all_to_all | solution.py:459
  13.2 0.0 copy-done.3
  13.2 3.3 %copy.7 = bf16[3,9,36864]{2,1,0:T(8,128)(2,1)} copy(bf16[3,9,36864]{2,0,1:T(4,128)(2,1)S(1)} %copy-done.3) | data formatting | bytes 3981312 | tf_op args[2]
  16.5 4.6 %reshape.80.w_ref = bf16[27,192,192]{2,1,0:T(8,128)(2,1)S(1)} reshape(bf16[3,9,36864]{2,1,0:T(8,128)(2,1)} %copy.7) | data formatting | bytes 3981312 | tf_op jit(solution)/shard_map/reshape | solution.py:460
  21.1 0.1 fusion.order_ref
  21.2 7.2 %all-to-all-done.recv_hbm = bf16[16,288,128]{2,1,0:T(8,128)(2,1)} async-done(((bf16[16,288,128]{2,1,0:T(8,128)(2,1)}), bf16[16,288,128]{2,1,0:T(8,128)(2,1)}, u32[]{:S(2)}, u32[]{:S(2)}) %all-to-all-start) | async-done | bytes 1179680 | tf_op jit(solution)/shard_map/all_to_all | solution.py:459
  28.5 5.5 %shard_map.59 = (bf16[3,768,192]{2,1,0:T(8,128)(2,1)S(1)}, bf16[768,192]{1,0:T(8,128)(2,1)S(1)}, bf16[768,192]{1,0:T(8,128)(2,1)S(1)}, bf16[768,192]{1,0:T(8,128...) custom-call(bf16[16,288,128]{2,1,0:T(8,128)(2,1)} %all-to-all-done.recv_hbm, ...), custom_call_target="tpu_custom_call" | custom-call | flops 2038431744 | bytes 9000000 | tf_op jit(solution)/shard_map/pallas_call | solution.py:52
  34.0 2.5 %shard_map.60 = (bf16[27,96,192]{2,1,0:T(8,128)(2,1)S(1)}, bf16[27,96,192]{2,1,0:T(8,128)(2,1)S(1)}) custom-call(bf16[3,768,192]{2,1,0:T(8,128)(2,1)S(1)} %get-tuple-element.16.a0_ref, bf16[768,192]{1,0:T(8,128)(2,1)S(1)} %get-tuple-element.17.a1_ref, bf16[768,192]{1,0:T(8,128)(2,1)S(1)} %get-tuple-element.18.a2_ref, ...), custom_call_target="tpu_custom_call" | custom-call | flops 1528823808 | bytes 7000000 | tf_op jit(solution)/shard_map/pallas_call | solution.py:52
  36.5 1.9 %collective-permute-start = (bf16[27,96,192]{2,1,0:T(8,128)(2,1)S(1)}, bf16[27,96,192]{2,1,0:T(8,128)(2,1)S(1)}, u32[]{:S(2)}, u32[]{:S(2)}) collective-permute-start(bf16[27,96,192]{2,1,0:T(8,128)(2,1)S(1)} %get-tuple-element.23), channel_id=1, source_target_pairs={{0,16},{16,0},{1,17},{17,1},{2,18},{18,2},{3,19},{19,3},{4,20},{20... | collective-permute-start | bytes 2985992 | tf_op jit(solution)/shard_map/ppermute | solution.py:478
  38.4 0.8 shard_map.61.part_ref
  39.2 2.3 %collective-permute-done.got_ref = bf16[27,96,192]{2,1,0:T(8,128)(2,1)S(1)} collective-permute-done((bf16[27,96,192]{2,1,0:T(8,128)(2,1)S(1)}, bf16[27,96,192]{2,1,0:T(8,128)(2,1)S(1)}, u32[]{:S(2)}, u32[]{:S(2)}) %collective-permute-start) | collective-permute-done | bytes 995360 | tf_op jit(solution)/shard_map/ppermute | solution.py:478
  41.5 0.8 shard_map.62
  42.2 27.1 %all_to_all.15.got_ref = bf16[16,416,128]{2,1,0:T(8,128)(2,1)S(1)} all-to-all(bf16[16,416,128]{2,1,0:T(8,128)(2,1)S(1)} %shard_map.62), channel_id=1, replica_groups=mesh['z'=16,'core'=2,'x'=4,'y'=4] {'x','y'}, dimensions={0} | all-to-all | bytes 3407872 | tf_op jit(solution)/shard_map/all_to_all | solution.py:488
  69.3 0.0 copy-start
  69.3 0.9 shard_map.63
  70.2 0.0 copy-start.1
  70.2 0.8 copy-done.1
  71.1 15.6 %all-to-all-start.2 = ((bf16[16,16,128]{2,1,0:T(8,128)(2,1)}), bf16[16,16,128]{2,1,0:T(8,128)(2,1)S(1)}, u32[]{:S(2)}, u32[]{:S(2)}) async-start(bf16[16,16,128]{2,1,0:T(8,128)(2,1)} %get-tuple-element.28), calls=%async_computation.2 | async-start | bytes 131072 | tf_op jit(solution)/shard_map/all_to_all | solution.py:497
  86.7 0.0 copy-done
  86.7 0.0 copy-start.2
  86.7 1.1 %copy-done.2 = bf16[16,160,128]{2,1,0:T(8,128)(2,1)S(1)} copy-done((bf16[16,160,128]{2,1,0:T(8,128)(2,1)S(1)}, bf16[16,160,128]{2,1,0:T(8,128)(2,1)}, u32[]{:S(2)}) %copy-start.2) | copy-done | bytes 655384
  87.8 2.1 %shard_map.64 = (bf16[1,16,9216]{2,1,0:T(8,128)(2,1)}, bf16[1,16,9216]{2,1,0:T(8,128)(2,1)}) custom-call(bf16[16,160,128]{2,1,0:T(8,128)(2,1)S(1)} %copy-done.2, bf16[1,16,9216]{2,1,0:T(8,128)(2,1)S(1)} %copy-done, bf16[27,192,192]{2,1,0:T(8,128)(2,1)S(1)} %reshape.80.w_ref), custom_call_target="tpu_custom_call" | custom-call | flops 509607936 | bytes 3000000 | tf_op jit(solution)/shard_map/pallas_call | solution.py:52
  89.9 9.6 %all-to-all-done.2.refs_0_ = bf16[16,16,128]{2,1,0:T(8,128)(2,1)S(1)} async-done(((bf16[16,16,128]{2,1,0:T(8,128)(2,1)}), bf16[16,16,128]{2,1,0:T(8,128)(2,1)S(1)}, u32[]{:S(2)}, u32[]{:S(2)}) %all-to-all-start.2) | async-done | bytes 65568 | tf_op jit(solution)/shard_map/all_to_all | solution.py:497
  99.5 0.7 shard_map.65
  (1 shorter events, 0.0 us)
Async XLA Ops:
  0.6 12.6 %copy-start.3 = (bf16[3,9,36864]{2,0,1:T(4,128)(2,1)S(1)}, bf16[3,9,36864]{2,0,1:T(4,128)(2,1)}, u32[]{:S(2)}) copy-start(bf16[3,9,36864]{2,0,1:T(4,128)(2,1)} %param.5) | copy-start | bytes 5971972
  3.2 25.2 %all-to-all-start = ((bf16[16,288,128]{2,1,0:T(8,128)(2,1)}), bf16[16,288,128]{2,1,0:T(8,128)(2,1)}, u32[]{:S(2)}, u32[]{:S(2)}) async-start(bf16[16,288,128]{2,1,0:T(8,128)(2,1)} %shard_map.58), calls=%async_computation | async-start | bytes 2359296 | tf_op jit(solution)/shard_map/all_to_all | solution.py:459
  36.5 5.0 %collective-permute-start = (bf16[27,96,192]{2,1,0:T(8,128)(2,1)S(1)}, bf16[27,96,192]{2,1,0:T(8,128)(2,1)S(1)}, u32[]{:S(2)}, u32[]{:S(2)}) collective-permute-start(bf16[27,96,192]{2,1,0:T(8,128)(2,1)S(1)} %get-tuple-element.23), channel_id=1, source_target_pairs={{0,16},{16,0},{1,17},{17,1},{2,18},{18,2},{3,19},{19,3},{4,20},{20... | collective-permute-start | bytes 2985992 | tf_op jit(solution)/shard_map/ppermute | solution.py:478
  69.3 17.4 %copy-start = (bf16[1,16,9216]{2,1,0:T(8,128)(2,1)S(1)}, bf16[1,16,9216]{2,1,0:T(8,128)(2,1)}, u32[]{:S(2)}) copy-start(bf16[1,16,9216]{2,1,0:T(8,128)(2,1)} %x_ref.1) | copy-start | bytes 884740
  70.2 0.8 copy-start.1
  71.1 28.5 %all-to-all-start.2 = ((bf16[16,16,128]{2,1,0:T(8,128)(2,1)}), bf16[16,16,128]{2,1,0:T(8,128)(2,1)S(1)}, u32[]{:S(2)}, u32[]{:S(2)}) async-start(bf16[16,16,128]{2,1,0:T(8,128)(2,1)} %get-tuple-element.28), calls=%async_computation.2 | async-start | bytes 131072 | tf_op jit(solution)/shard_map/all_to_all | solution.py:497
  86.7 1.1 %copy-start.2 = (bf16[16,160,128]{2,1,0:T(8,128)(2,1)S(1)}, bf16[16,160,128]{2,1,0:T(8,128)(2,1)}, u32[]{:S(2)}) copy-start(bf16[16,160,128]{2,1,0:T(8,128)(2,1)} %copy-done.1) | copy-start | bytes 1966084

commit v3 on v2

--- a/solution.py
+++ b/solution.py
@@ -72,8 +72,7 @@
     ]
     for copy in copies:
         copy.start()
-    for copy in copies:
-        copy.wait()
+    copies[0].wait()
     act_ref[...] = gelu(x_ref[0].astype(F32)).astype(BF16)
 
     def column(load, w):
@@ -81,6 +80,7 @@
         base = 192 * (w % 2)
         return pair[:, base : base + 128], pair[:, base + 128 : base + 192]
 
+    copies[1].wait()
     nothing = jnp.zeros((16, 128), BF16), jnp.zeros((16, 64), BF16)
     act, raw, cot, leaving = [], [], [], []
     for w in range(WIDTH):
@@ -152,12 +152,12 @@
     pltpu.VMEM((GROUPS, HEIGHT + 64, CH), BF16),
     pltpu.VMEM((CELLS, CH), F32),
     pltpu.VMEM((CELLS, CH), F32),
-    pltpu.SemaphoreType.DMA((3,)),
+    pltpu.SemaphoreType.DMA((4,)),
 )
 
 
 def main_kernel(
-    recv_hbm, w_ref, a0_ref, a1_ref, a2_ref, g1_ref, g2_ref, g3_ref, s2_ref,
+    recv_hbm, w_ref, a0_ref, a1_ref, a2_ref, g1_ref, g2_ref, g3_ref, s2_ref, first_hbm,
     recv_ref, a0p, a1p, g2p, g3p, slope1, slope2, sems,
 ):
     def rows_copy(n, lo, hi):
@@ -167,6 +167,7 @@
         part.start()
         return part
 
+    first = pltpu.make_async_copy(w_ref.at[0:9], first_hbm, sems.at[3])
     moving = [rows_copy(0, 0, 144), rows_copy(1, 192, 288), rows_copy(2, 144, 192)]
 
     def block(k):
@@ -178,6 +179,7 @@
     for ref, pad in ((a1p, 16), (g2p, 16), (g3p, 32)):
         clear_edges(ref, pad)
 
+    first.start()
     moving[0].wait()
     moving[1].wait()
     state = []
@@ -234,6 +236,7 @@
         rows = slice(HEIGHT * a, HEIGHT * (a + 1))
         grad = g2_ref[rows, :].astype(F32) + back[a] * slope1[rows, :]
         g1_ref[rows, :] = grad.astype(BF16)
+    first.wait()
 
 
 def final_kernel(a2_ref, s2_ref, g1_ref, w_ref, send_ref, a2p):
@@ -273,8 +276,10 @@
     order = order_ref[...]
 
     def store(tap, value):
-        keep_ref[tap] = value[0:96, :].astype(BF16)
-        give_ref[tap] = value[96:192, :].astype(BF16)
+        for ref, at in ((keep_ref, 0), (give_ref, 96)):
+            ref[tap, 0:96, :] = value[at : at + 96, 0:128].astype(BF16)
+            both = [value[at + 48 * h : at + 48 * h + 48, 128:192] for h in range(2)]
+            ref[tap, 96:144, :] = jnp.concatenate(both, axis=1).astype(BF16)
 
     def spread_grad(layer, act_ref, grad_ref, width, step):
         for a in range(GROUPS):
@@ -329,7 +334,12 @@
                 for tap in range(7 * group, min(7 * group + 7, 27)):
                     for j, lo, hi in pieces:
                         at = 48 * h + 16 * j
-                        parts.append(total[tap, at : at + 16, lo:hi])
+                        if lo < 128:
+                            parts.append(total[tap, at : at + 16, lo : min(hi, 128)])
+                        if hi > 128:
+                            at = 96 + 16 * j
+                            first = 64 * h + max(lo, 128) - 128
+                            parts.append(total[tap, at : at + 16, first : 64 * h + hi - 128])
                 parts.append(jnp.zeros((16, 80 if group == 3 else 8), BF16))
                 line = jnp.concatenate(parts, axis=1)
                 for n in range(4):
@@ -337,16 +347,13 @@
                     send_ref[8 * h + t, at : at + 16, :] = line[:, 128 * n : 128 * n + 128]
 
 
-def gather_kernel(got_ref, send_ref, rest_hbm, total_ref, sem):
-    rest = pltpu.make_async_copy(got_ref.at[:, 256:416, :], rest_hbm, sem)
-    rest.start()
+def gather_kernel(got_ref, send_ref, total_ref):
     total = got_ref[0, 0:256, :].astype(F32)
     for s in range(1, 16):
         total = total + got_ref[s, 0:256, :].astype(F32)
     total_ref[...] = total
     for z in range(16):
         send_ref[z] = total_ref[pl.ds(z, 16, stride=16), :].astype(BF16)
-    rest.wait()
 
 
 def finish_kernel(scale, got_ref, out_ref):
@@ -365,9 +372,15 @@
         out_ref[tap : tap + 1, :] = parts[0] if len(parts) == 1 else jnp.concatenate(parts, axis=1)
 
 
-def last_kernel(recv_ref, x_ref, w_ref, out_ref, grad_ref, padded, slope_ref, grads_ref):
+def last_kernel(
+    w_hbm, recv_ref, x_ref, out_ref, grad_ref, w_ref, padded, slope_ref, grads_ref, sem
+):
+    weights = pltpu.make_async_copy(w_hbm, w_ref, sem)
+    weights.start()
+
     def tile(k):
-        return recv_ref[:, 16 * k : 16 * k + 16, :].reshape(HEIGHT, 128).astype(F32)
+        at = 256 + 16 * k
+        return recv_ref[:, at : at + 16, :].reshape(HEIGHT, 128).astype(F32)
 
     lows = [tile(k) for k in range(6)]
     highs = []
@@ -416,6 +429,7 @@
         slope_ref[32 * p : 32 * p + 16, :] = slope[:, 0:192]
         slope_ref[32 * p + 16 : 32 * p + 32, :] = slope[:, 192:384]
 
+    weights.wait()
     cells, taps = [], []
     for i in range(3):
         for j in range(3):
@@ -458,18 +472,19 @@
     )
     recv = lax.all_to_all(send, SPACE, 0, 0, tiled=True)
     kernels = weights.reshape(27, CH, CH)
-    a0, a1, a2, g1, g2, g3, s2 = call(
+    a0, a1, a2, g1, g2, g3, s2, first = call(
         main_kernel,
-        (shape(3, CELLS, CH),) + (shape(CELLS, CH),) * 6,
+        (shape(3, CELLS, CH),) + (shape(CELLS, CH),) * 6 + (shape(9, CH, CH),),
         kernels,
         remain=(recv,),
         scratch=MAIN_SCRATCH,
+        apart=1,
         flops=4 * 2 * CELLS * 9 * CH * CH,
         moved=9000000,
     )
     keep, give = call(
         wgrad_kernel,
-        (shape(27, 96, CH), shape(27, 96, CH)),
+        (shape(27, 144, 128), shape(27, 144, 128)),
         a0, a1, a2, g1, g2, g3, order,
         scratch=(pltpu.VMEM((GROUPS, HEIGHT + 64, CH), BF16), pltpu.VMEM((CH, CELLS), BF16)),
         flops=3 * 2 * CELLS * 9 * CH * CH,
@@ -486,13 +501,12 @@
     )
     send = call(split_kernel, shape(16, 416, 128), keep, got, part, moved=5000000)
     back = lax.all_to_all(send, SPACE, 0, 0, tiled=True)
-    send, rest = call(
+    send = call(
         gather_kernel,
-        (shape(16, 16, 128), shape(16, 160, 128)),
+        shape(16, 16, 128),
         back,
-        scratch=(pltpu.VMEM((256, 128), F32), pltpu.SemaphoreType.DMA),
+        scratch=(pltpu.VMEM((256, 128), F32),),
         moved=2500000,
-        apart=1,
     )
     got = lax.all_to_all(send, "z", 0, 0, tiled=True)
     weight_grad = call(
@@ -501,11 +515,14 @@
     outputs, input_grad = call(
         last_kernel,
         (shape(1, ROWS, 9216), shape(1, ROWS, 9216)),
-        rest, inputs, kernels,
+        back, inputs,
+        remain=(first,),
         scratch=(
+            pltpu.VMEM((9, CH, CH), BF16),
             pltpu.VMEM((3, CELLS + 32, CH), BF16),
             pltpu.VMEM((CELLS, CH), F32),
             pltpu.VMEM((CELLS, CH), F32),
+            pltpu.SemaphoreType.DMA,
         ),
         flops=2 * CELLS * 9 * CH * CH,
         moved=3000000,

time: 101 us -> 99.6 us (0.986)
  the two profiles are of different devices: /device:TPU:8 before, /device:TPU:2 now
where the time goes in v3:
time: 99.6 us; the launch traced here: 99.2 us
  blocking collectives  28.1 us (28%)
  starting transfers between devices  27.6 us (28%)
  waiting for transfers between devices  17.4 us (17%)
  Pallas kernels  16.7 us (17%)
  local copies, waits for them, and re-layouts  7.93 us (8%)
    all_to_all x1, blocking collectives, body(): back = lax.all_to_all(send, SPACE, 0, 0, tiled=True)  28.1 us
    pallas_call x8, Pallas kernels, call(): pl.pallas_call(kernel, out_shape=out_shape, in_specs=[pl.BlockSpec(memory...  16.7 us
    all_to_all x1, starting transfers between devices, body(): got = lax.all_to_all(send, 'z', 0, 0, tiled=True)  15.6 us
    all_to_all x1, starting transfers between devices, body(): recv = lax.all_to_all(send, SPACE, 0, 0, tiled=True)  10.1 us
    all_to_all x1, waiting for transfers between devices, body(): got = lax.all_to_all(send, 'z', 0, 0, tiled=True)  10 us
    all_to_all x1, waiting for transfers between devices, body(): recv = lax.all_to_all(send, SPACE, 0, 0, tiled=True)  5.57 us
    reshape x1, local copies, waits for them, and re-layouts, body(): kernels = weights.reshape(27, CH, CH)  4.65 us
    unnamed x7, local copies, waits for them, and re-layouts  3.28 us
  transfers between devices with their start and end apart: 3, of which 3 were waited for; matrix products, arithmetic and copies ran while one was open for 9% of the time, Pallas kernels for 4%

profile of v3, /device:TPU:2, one launch (start us, length us, event | category | flops | bytes accessed | tf_op | source)
XLA Modules:
  0.0 99.2 jit_solution(2722521078226797632)
XLA Ops:
  0.6 0.0 copy-start.2
  0.6 2.6 %shard_map.58 = bf16[16,288,128]{2,1,0:T(8,128)(2,1)} custom-call(bf16[1,16,9216]{2,1,0:T(8,128)(2,1)} %x_ref.1, bf16[1,16,9216]{2,1,0:T(8,128)(2,1)} %c_hbm.1), custom_call_target="tpu_custom_call" | custom-call | bytes 2500000 | tf_op jit(solution)/shard_map/pallas_call | solution.py:52
  3.3 10.1 %all-to-all-start = ((bf16[16,288,128]{2,1,0:T(8,128)(2,1)}), bf16[16,288,128]{2,1,0:T(8,128)(2,1)}, u32[]{:S(2)}, u32[]{:S(2)}) async-start(bf16[16,288,128]{2,1,0:T(8,128)(2,1)} %shard_map.58), calls=%async_computation | async-start | bytes 2359296 | tf_op jit(solution)/shard_map/all_to_all | solution.py:473
  13.3 0.0 copy-done.2
  13.4 3.3 %copy.7 = bf16[3,9,36864]{2,1,0:T(8,128)(2,1)} copy(bf16[3,9,36864]{2,0,1:T(4,128)(2,1)S(1)} %copy-done.2) | data formatting | bytes 3981312 | tf_op args[2]
  16.6 4.6 %reshape.80.w_ref = bf16[27,192,192]{2,1,0:T(8,128)(2,1)S(1)} reshape(bf16[3,9,36864]{2,1,0:T(8,128)(2,1)} %copy.7) | data formatting | bytes 3981312 | tf_op jit(solution)/shard_map/reshape | solution.py:474
  21.3 0.7 fusion.order_ref
  22.0 5.6 %all-to-all-done.recv_hbm = bf16[16,288,128]{2,1,0:T(8,128)(2,1)} async-done(((bf16[16,288,128]{2,1,0:T(8,128)(2,1)}), bf16[16,288,128]{2,1,0:T(8,128)(2,1)}, u32[]{:S(2)}, u32[]{:S(2)}) %all-to-all-start) | async-done | bytes 1179680 | tf_op jit(solution)/shard_map/all_to_all | solution.py:473
  27.6 0.0 copy-start.1
  27.6 5.6 %shard_map.59 = (bf16[3,768,192]{2,1,0:T(8,128)(2,1)S(1)}, bf16[768,192]{1,0:T(8,128)(2,1)S(1)}, bf16[768,192]{1,0:T(8,128)(2,1)S(1)}, bf16[768,192]{1,0:T(8,128...) custom-call(bf16[16,288,128]{2,1,0:T(8,128)(2,1)} %all-to-all-done.r, ...), custom_call_target="tpu_custom_call" | custom-call | flops 2038431744 | bytes 9000000 | tf_op jit(solution)/shard_map/pallas_call | solution.py:52
  33.2 0.0 copy-done.1
  33.2 2.6 %shard_map.60 = (bf16[27,144,128]{2,1,0:T(8,128)(2,1)S(1)}, bf16[27,144,128]{2,1,0:T(8,128)(2,1)S(1)}) custom-call(bf16[3,768,192]{2,1,0:T(8,128)(2,1)S(1)} %get-tuple-element.16.a0_ref, bf16[768,192]{1,0:T(8,128)(2,1)S(1)} %get-tuple-element.17.a1_ref, bf16[768,192]{1,0:T(8,128)(2,1)S(1)} %get-tuple-element.18.a2_ref, ...), custom_call_target="tpu_custom_call" | custom-call | flops 1528823808 | bytes 7000000 | tf_op jit(solution)/shard_map/pallas_call | solution.py:52
  35.8 1.9 %collective-permute-start = (bf16[27,144,128]{2,1,0:T(8,128)(2,1)S(1)}, bf16[27,144,128]{2,1,0:T(8,128)(2,1)S(1)}, u32[]{:S(2)}, u32[]{:S(2)}) collective-permute-start(bf16[27,144,128]{2,1,0:T(8,128)(2,1)S(1)} %get-tuple-element.23), channel_id=1, source_target_pairs={{0,16},{16,0},{1,17},{17,1},{2,18},{18,2},{3,19},{19,3},{4,20},{20... | collective-permute-start | bytes 2985992 | tf_op jit(solution)/shard_map/ppermute | solution.py:493
  37.8 0.8 shard_map.61.part_ref
  38.5 1.8 %collective-permute-done.got_ref = bf16[27,144,128]{2,1,0:T(8,128)(2,1)S(1)} collective-permute-done((bf16[27,144,128]{2,1,0:T(8,128)(2,1)S(1)}, bf16[27,144,128]{2,1,0:T(8,128)(2,1)S(1)}, u32[]{:S(2)}, u32[]{:S(2)}) %collective-permute-start) | collective-permute-done | bytes 995360 | tf_op jit(solution)/shard_map/ppermute | solution.py:493
  40.3 0.8 shard_map.62
  41.1 28.1 %all_to_all.15.recv_ref.got_ref = bf16[16,416,128]{2,1,0:T(8,128)(2,1)S(1)} all-to-all(bf16[16,416,128]{2,1,0:T(8,128)(2,1)S(1)} %shard_map.62), channel_id=1, replica_groups=mesh['z'=16,'core'=2,'x'=4,'y'=4] {'x','y'}, dimensions={0} | all-to-all | bytes 3407872 | tf_op jit(solution)/shard_map/all_to_all | solution.py:503
  69.2 0.0 copy-start
  69.2 0.8 shard_map.64
  70.0 15.6 %all-to-all-start.2 = ((bf16[16,16,128]{2,1,0:T(8,128)(2,1)}), bf16[16,16,128]{2,1,0:T(8,128)(2,1)S(1)}, u32[]{:S(2)}, u32[]{:S(2)}) async-start(bf16[16,16,128]{2,1,0:T(8,128)(2,1)} %shard_map.64), calls=%async_computation.2 | async-start | bytes 131072 | tf_op jit(solution)/shard_map/all_to_all | solution.py:511
  85.6 0.0 copy-done
  85.6 2.8 %shard_map.63 = (bf16[1,16,9216]{2,1,0:T(8,128)(2,1)}, bf16[1,16,9216]{2,1,0:T(8,128)(2,1)}) custom-call(bf16[9,192,192]{2,1,0:T(8,128)(2,1)S(1)} %get-tuple-element.15.w_hbm, bf16[16,416,128]{2,1,0:T(8,128)(2,1)S(1)} %all_to_all.15.recv_ref.got_ref, bf16[1,16,9216]{2,1,0:T(8,128)(2,1)S(1)} %copy-done), custom_call_target="tpu_custom_call" | custom-call | flops 509607936 | bytes 3000000 | tf_op jit(solution)/shard_map/pallas_call | solution.py:52
  88.4 10.0 %all-to-all-done.2.refs_0_ = bf16[16,16,128]{2,1,0:T(8,128)(2,1)S(1)} async-done(((bf16[16,16,128]{2,1,0:T(8,128)(2,1)}), bf16[16,16,128]{2,1,0:T(8,128)(2,1)S(1)}, u32[]{:S(2)}, u32[]{:S(2)}) %all-to-all-start.2) | async-done | bytes 65568 | tf_op jit(solution)/shard_map/all_to_all | solution.py:511
  98.5 0.7 shard_map.65
  (1 shorter events, 0.0 us)
Async XLA Ops:
  0.6 12.7 %copy-start.2 = (bf16[3,9,36864]{2,0,1:T(4,128)(2,1)S(1)}, bf16[3,9,36864]{2,0,1:T(4,128)(2,1)}, u32[]{:S(2)}) copy-start(bf16[3,9,36864]{2,0,1:T(4,128)(2,1)} %param.5) | copy-start | bytes 5971972
  3.3 24.3 %all-to-all-start = ((bf16[16,288,128]{2,1,0:T(8,128)(2,1)}), bf16[16,288,128]{2,1,0:T(8,128)(2,1)}, u32[]{:S(2)}, u32[]{:S(2)}) async-start(bf16[16,288,128]{2,1,0:T(8,128)(2,1)} %shard_map.58), calls=%async_computation | async-start | bytes 2359296 | tf_op jit(solution)/shard_map/all_to_all | solution.py:473
  27.6 5.6 %copy-start.1 = (bf16[192,192]{1,0:T(8,128)(2,1)S(1)}, bf16[192,192]{1,0:T(8,128)(2,1)}, u32[]{:S(2)}) copy-start(bf16[192,192]{1,0:T(8,128)(2,1)} %fusion.order_ref) | copy-start | bytes 221188
  35.8 4.5 %collective-permute-start = (bf16[27,144,128]{2,1,0:T(8,128)(2,1)S(1)}, bf16[27,144,128]{2,1,0:T(8,128)(2,1)S(1)}, u32[]{:S(2)}, u32[]{:S(2)}) collective-permute-start(bf16[27,144,128]{2,1,0:T(8,128)(2,1)S(1)} %get-tuple-element.23), channel_id=1, source_target_pairs={{0,16},{16,0},{1,17},{17,1},{2,18},{18,2},{3,19},{19,3},{4,20},{20... | collective-permute-start | bytes 2985992 | tf_op jit(solution)/shard_map/ppermute | solution.py:493
  69.2 16.5 %copy-start = (bf16[1,16,9216]{2,1,0:T(8,128)(2,1)S(1)}, bf16[1,16,9216]{2,1,0:T(8,128)(2,1)}, u32[]{:S(2)}) copy-start(bf16[1,16,9216]{2,1,0:T(8,128)(2,1)} %x_ref.1) | copy-start | bytes 884740
  70.0 28.5 %all-to-all-start.2 = ((bf16[16,16,128]{2,1,0:T(8,128)(2,1)}), bf16[16,16,128]{2,1,0:T(8,128)(2,1)S(1)}, u32[]{:S(2)}, u32[]{:S(2)}) async-start(bf16[16,16,128]{2,1,0:T(8,128)(2,1)} %shard_map.64), calls=%async_computation.2 | async-start | bytes 131072 | tf_op jit(solution)/shard_map/all_to_all | solution.py:511

commit v4 on v3

--- a/solution.py
+++ b/solution.py
@@ -10,7 +10,9 @@
 
 
 DP = ("z", "core")
-SPACE = ("x", "y")
+SPACE = ("space",)
+Z_ORDER = tuple((z + 11) % 16 for z in range(16))
+TURNED = tuple(4 * ((s // 4 + 2) % 4) + (s + 2) % 4 for s in range(16))
 CH = 192
 ROWS = 16
 WIDTH = 48
@@ -33,8 +35,9 @@
     square = x * x
     tanh = jnp.tanh(GELU_A * (x + GELU_B * (x * square)))
     cdf = 0.5 * (1.0 + tanh)
-    slope = cdf + (0.5 * x) * ((1.0 - tanh * tanh) * (GELU_A + (3.0 * GELU_A * GELU_B) * square))
-    return x * cdf, slope
+    act = x * cdf
+    slope = cdf + (act * (1.0 - cdf)) * (2.0 * GELU_A + (6.0 * GELU_A * GELU_B) * square)
+    return act, slope
 
 
 def dot(a, b):
@@ -61,26 +64,44 @@
     )(*remain, *args)
 
 
+def plane_exchange(value):
+    groups = [list(TURNED)]
+    return lax.all_to_all(value, "space", 0, 0, axis_index_groups=groups, tiled=True)
+
+
 def shape(*dims, dtype=BF16):
     return jax.ShapeDtypeStruct(dims, dtype)
 
 
+PACK_SCRATCH = (
+    pltpu.VMEM((1, ROWS, 9216), BF16),
+    pltpu.VMEM((1, ROWS, 9216), BF16),
+    pltpu.VMEM((ROWS, 9216), BF16),
+    pltpu.VMEM((16, 288, 128), BF16),
+    pltpu.SemaphoreType.DMA((6,)),
+    pltpu.SemaphoreType.DMA((16,)),
+)
+
+
 def pack_kernel(x_hbm, c_hbm, send_hbm, x_ref, c_ref, act_ref, send_ref, sems, send_sems):
-    copies = [
-        pltpu.make_async_copy(x_hbm, x_ref, sems.at[0]),
-        pltpu.make_async_copy(c_hbm, c_ref, sems.at[1]),
-    ]
-    for copy in copies:
-        copy.start()
-    copies[0].wait()
-    act_ref[...] = gelu(x_ref[0].astype(F32)).astype(BF16)
+    copies = []
+    for n in range(6):
+        source, target = ((x_hbm, x_ref), (c_hbm, c_ref))[n // 3]
+        part = pl.ds(3072 * (n % 3), 3072)
+        copies.append(pltpu.make_async_copy(source.at[:, :, part], target.at[:, :, part], sems.at[n]))
+        copies[n].start()
+    for n in range(3):
+        copies[n].wait()
+        part = slice(3072 * n, 3072 * (n + 1))
+        act_ref[:, part] = gelu(x_ref[0, :, part].astype(F32)).astype(BF16)
 
     def column(load, w):
         pair = load(384 * (w // 2))
         base = 192 * (w % 2)
         return pair[:, base : base + 128], pair[:, base + 128 : base + 192]
 
-    copies[1].wait()
+    for copy in copies[3:]:
+        copy.wait()
     nothing = jnp.zeros((16, 128), BF16), jnp.zeros((16, 64), BF16)
     act, raw, cot, leaving = [], [], [], []
     for w in range(WIDTH):
@@ -105,7 +126,7 @@
         for k in range(6):
             both = jnp.concatenate([blocks[2 * k][1], blocks[2 * k + 1][1]], axis=1)
             send_ref[b, 192 + 16 * k : 208 + 16 * k, :] = both
-        leaving.append(pltpu.make_async_copy(send_ref.at[b], send_hbm.at[b], send_sems.at[b]))
+        leaving.append(pltpu.make_async_copy(send_ref.at[b], send_hbm.at[TURNED[b]], send_sems.at[b]))
         leaving[b].start()
     for copy in leaving:
         copy.wait()
@@ -118,24 +139,28 @@
     return jnp.where(keep, rolled, 0.0)
 
 
-def spread_conv(padded, w_ref, layer, width, step, transposed):
-    totals = []
-    for a in range(GROUPS):
-        cells, taps = [], []
-        for j in range(3):
-            src = a + ((1 - j) * step if transposed else (j - 1) * step)
-            if not 0 <= src < GROUPS:
-                continue
-            for i in range(3):
-                at = width * (2 - i) if transposed else width * i
-                cells.append(padded[src, at : at + HEIGHT, :])
-                taps.append(w_ref[9 * layer + 3 * i + j])
-        cells = jnp.concatenate(cells, axis=1)
-        if transposed:
-            totals.append(dot_t(cells, jnp.concatenate(taps, axis=1)))
-        else:
-            totals.append(dot(cells, jnp.concatenate(taps, axis=0)))
-    return totals
+def spread_conv_at(a, padded, w_ref, layer, width, step, transposed):
+    cells, taps = [], []
+    for j in range(3):
+        src = a + ((1 - j) * step if transposed else (j - 1) * step)
+        if not 0 <= src < GROUPS:
+            continue
+        for i in range(3):
+            at = width * (2 - i) if transposed else width * i
+            cells.append(padded[src, at : at + HEIGHT, :])
+            taps.append(w_ref[9 * layer + 3 * i + j])
+    cells = jnp.concatenate(cells, axis=1)
+    if transposed:
+        return dot_t(cells, jnp.concatenate(taps, axis=1))
+    return dot(cells, jnp.concatenate(taps, axis=0))
+
+
+def spread_conv(*args):
+    return [spread_conv_at(a, *args) for a in range(GROUPS)]
+
+
+def slabs(ref, at):
+    return jnp.concatenate([ref[TURNED[s], at : at + 16, :] for s in range(16)], axis=0)
 
 
 def clear_edges(ref, pad):
@@ -171,9 +196,8 @@
     moving = [rows_copy(0, 0, 144), rows_copy(1, 192, 288), rows_copy(2, 144, 192)]
 
     def block(k):
-        lo = recv_ref[:, 16 * k : 16 * k + 16, :].reshape(HEIGHT, 128)
-        at = 192 + 16 * (k // 2)
-        hi = recv_ref[:, at : at + 16, :].reshape(HEIGHT, 128)[:, 64 * (k % 2) : 64 * (k % 2) + 64]
+        lo = slabs(recv_ref, 16 * k)
+        hi = slabs(recv_ref, 192 + 16 * (k // 2))[:, 64 * (k % 2) : 64 * (k % 2) + 64]
         return jnp.concatenate([lo, hi], axis=1)
 
     for ref, pad in ((a1p, 16), (g2p, 16), (g3p, 32)):
@@ -203,8 +227,8 @@
         cot = block(9 + a)
         g3_ref[HEIGHT * a : HEIGHT * (a + 1), :] = cot
         g3p[a, 32 : 32 + HEIGHT, :] = cot
-    back = spread_conv(g3p, w_ref, 2, 32, 2, True)
-    for a in range(GROUPS):
+
+    def first_state(a):
         rows = slice(HEIGHT * a, HEIGHT * (a + 1))
         branch = shifted_rows(sums[0][a], -1) + sums[1][a] + shifted_rows(sums[2][a], 1)
         state[a] = (state[a].astype(F32) + branch).astype(BF16)
@@ -214,28 +238,42 @@
         a1_ref[rows, :] = act
         a1p[a, 16 : 16 + HEIGHT, :] = act
 
-    branch = spread_conv(a1p, w_ref, 1, 16, 1, False)
-    for a in range(GROUPS):
+    def second_state(a, branch, back):
         rows = slice(HEIGHT * a, HEIGHT * (a + 1))
-        state[a] = (state[a].astype(F32) + branch[a]).astype(BF16)
+        state[a] = (state[a].astype(F32) + branch).astype(BF16)
         act, slope = gelu_and_slope(state[a].astype(F32))
-        act = act.astype(BF16)
-        slope2[rows, :] = slope
-        a2_ref[rows, :] = act
+        a2_ref[rows, :] = act.astype(BF16)
         s2_ref[rows, :] = state[a]
-
-    for a in range(GROUPS):
-        rows = slice(HEIGHT * a, HEIGHT * (a + 1))
-        grad = g3_ref[rows, :].astype(F32) + back[a] * slope2[rows, :]
-        grad = grad.astype(BF16)
+        grad = (g3_ref[rows, :].astype(F32) + back * slope).astype(BF16)
         g2_ref[rows, :] = grad
         g2p[a, 16 : 16 + HEIGHT, :] = grad
 
-    back = spread_conv(g2p, w_ref, 1, 16, 1, True)
-    for a in range(GROUPS):
+    def third_grad(a, back):
         rows = slice(HEIGHT * a, HEIGHT * (a + 1))
-        grad = g2_ref[rows, :].astype(F32) + back[a] * slope1[rows, :]
+        grad = g2_ref[rows, :].astype(F32) + back * slope1[rows, :]
         g1_ref[rows, :] = grad.astype(BF16)
+
+    fwd = (a1p, w_ref, 1, 16, 1, False)
+    far = (g3p, w_ref, 2, 32, 2, True)
+    near = (g2p, w_ref, 1, 16, 1, True)
+    back0 = spread_conv_at(0, *far)
+    first_state(0)
+    first_state(1)
+    branch0 = spread_conv_at(0, *fwd)
+    first_state(2)
+    branch1 = spread_conv_at(1, *fwd)
+    second_state(0, branch0, back0)
+    back1 = spread_conv_at(1, *far)
+    branch2 = spread_conv_at(2, *fwd)
+    second_state(1, branch1, back1)
+    back2 = spread_conv_at(2, *far)
+    near0 = spread_conv_at(0, *near)
+    second_state(2, branch2, back2)
+    third_grad(0, near0)
+    near1 = spread_conv_at(1, *near)
+    near2 = spread_conv_at(2, *near)
+    third_grad(1, near1)
+    third_grad(2, near2)
     first.wait()
 
 
@@ -306,10 +344,11 @@
         shifted[2].append(shifted_rows(rows, -1).astype(BF16))
     shifted[0] = jnp.concatenate(shifted[0], axis=0)
     shifted[2] = jnp.concatenate(shifted[2], axis=0)
-    for j in range(3):
-        acts[...] = dot_t(order, a0_ref[j]).astype(BF16)
-        for i in range(3):
-            store(3 * i + j, dot(acts[...], shifted[i]))
+    stack = jnp.concatenate([dot_t(order, a0_ref[j]).astype(BF16) for j in range(3)], axis=0)
+    for i in range(3):
+        value = dot(stack, shifted[i])
+        for j in range(3):
+            store(3 * i + j, value[CH * j : CH * (j + 1)])
 
 
 PIECES = (
@@ -325,7 +364,9 @@
 
 
 def split_kernel(keep_ref, got_ref, part_ref, send_ref):
-    send_ref[:, 256:416, :] = part_ref[...]
+    for s in range(16):
+        send_ref[TURNED[s], 256:416, :] = part_ref[s]
+
     total = (keep_ref[...].astype(F32) + got_ref[...].astype(F32)).astype(BF16)
     for h in range(2):
         for t, pieces in enumerate(PIECES):
@@ -344,7 +385,7 @@
                 line = jnp.concatenate(parts, axis=1)
                 for n in range(4):
                     at = 64 * group + 16 * n
-                    send_ref[8 * h + t, at : at + 16, :] = line[:, 128 * n : 128 * n + 128]
+                    send_ref[TURNED[8 * h + t], at : at + 16, :] = line[:, 128 * n : 128 * n + 128]
 
 
 def gather_kernel(got_ref, send_ref, total_ref):
@@ -352,8 +393,8 @@
     for s in range(1, 16):
         total = total + got_ref[s, 0:256, :].astype(F32)
     total_ref[...] = total
-    for z in range(16):
-        send_ref[z] = total_ref[pl.ds(z, 16, stride=16), :].astype(BF16)
+    for place, z in enumerate(Z_ORDER):
+        send_ref[place] = total_ref[pl.ds(z, 16, stride=16), :].astype(BF16)
 
 
 def finish_kernel(scale, got_ref, out_ref):
@@ -379,8 +420,7 @@
     weights.start()
 
     def tile(k):
-        at = 256 + 16 * k
-        return recv_ref[:, at : at + 16, :].reshape(HEIGHT, 128).astype(F32)
+        return slabs(recv_ref, 256 + 16 * k).astype(F32)
 
     lows = [tile(k) for k in range(6)]
     highs = []
@@ -458,19 +498,12 @@
         pack_kernel,
         shape(16, 288, 128),
         remain=(inputs, cotangent),
-        scratch=(
-            pltpu.VMEM((1, ROWS, 9216), BF16),
-            pltpu.VMEM((1, ROWS, 9216), BF16),
-            pltpu.VMEM((ROWS, 9216), BF16),
-            pltpu.VMEM((16, 288, 128), BF16),
-            pltpu.SemaphoreType.DMA((2,)),
-            pltpu.SemaphoreType.DMA((16,)),
-        ),
+        scratch=PACK_SCRATCH,
         moved=2500000,
         apart=1,
         limit=VMEM_MOST,
     )
-    recv = lax.all_to_all(send, SPACE, 0, 0, tiled=True)
+    recv = plane_exchange(send)
     kernels = weights.reshape(27, CH, CH)
     a0, a1, a2, g1, g2, g3, s2, first = call(
         main_kernel,
@@ -500,7 +533,7 @@
         moved=4500000,
     )
     send = call(split_kernel, shape(16, 416, 128), keep, got, part, moved=5000000)
-    back = lax.all_to_all(send, SPACE, 0, 0, tiled=True)
+    back = plane_exchange(send)
     send = call(
         gather_kernel,
         shape(16, 16, 128),
@@ -508,7 +541,7 @@
         scratch=(pltpu.VMEM((256, 128), F32),),
         moved=2500000,
     )
-    got = lax.all_to_all(send, "z", 0, 0, tiled=True)
+    got = lax.all_to_all(send, "z", 0, 0, axis_index_groups=[list(Z_ORDER)], tiled=True)
     weight_grad = call(
         lambda *refs: finish_kernel(scale, *refs), shape(27, 72, dtype=F32), got, moved=150000
     )
@@ -531,7 +564,7 @@
 
 
 def solution(mesh):
-    devices = mesh.devices.reshape(16, 2, 4, 4)
+    devices = mesh.devices.reshape(16, 2, 16)
     wide = Mesh(devices, DP + SPACE)
     placed = (P(DP, SPACE, None), P(DP, SPACE, None), P())
     return jax.shard_map(

time: 99.6 us -> 92.5 us (0.929)
  the two profiles are of different devices: /device:TPU:2 before, /device:TPU:8 now
where the time goes in v4:
time: 92.5 us; the launch traced here: 92.1 us
  starting transfers between devices  29.6 us (32%)
  blocking collectives  26.6 us (29%)
  Pallas kernels  16.3 us (18%)
  waiting for transfers between devices  10.1 us (11%)
  local copies, waits for them, and re-layouts  7.93 us (9%)
    all_to_all x1, blocking collectives, plane_exchange(): lax.all_to_all(value, 'space', 0, 0, axis_index_groups=groups, tiled=True)  26.6 us
    all_to_all x1, starting transfers between devices, body(): lax.all_to_all(send, 'z', 0, 0, axis_index_groups=[list(Z_ORDER)], tiled=...  16.7 us
    pallas_call x8, Pallas kernels, call(): pl.pallas_call(kernel, out_shape=out_shape, in_specs=[pl.BlockSpec(memory...  16.3 us
    all_to_all x1, starting transfers between devices, plane_exchange(): lax.all_to_all(value, 'space', 0, 0, axis_index_groups=groups, tiled=True)  11 us
    all_to_all x1, waiting for transfers between devices, plane_exchange(): lax.all_to_all(value, 'space', 0, 0, axis_index_groups=groups, tiled=True)  4.71 us
    reshape x1, local copies, waits for them, and re-layouts, body(): kernels = weights.reshape(27, CH, CH)  4.65 us
    all_to_all x1, waiting for transfers between devices, body(): lax.all_to_all(send, 'z', 0, 0, axis_index_groups=[list(Z_ORDER)], tiled=...  3.59 us
    unnamed x7, local copies, waits for them, and re-layouts  3.28 us
  transfers between devices with their start and end apart: 3, of which 3 were waited for; matrix products, arithmetic and copies ran while one was open for 9% of the time, Pallas kernels for 4%

profile of v4, /device:TPU:8, one launch (start us, length us, event | category | flops | bytes accessed | tf_op | source)
XLA Modules:
  0.0 92.1 jit_solution(9217015061069788345)
XLA Ops:
  0.6 0.0 copy-start.2
  0.6 2.6 %shard_map.58 = bf16[16,288,128]{2,1,0:T(8,128)(2,1)} custom-call(bf16[1,16,9216]{2,1,0:T(8,128)(2,1)} %x_ref.1, bf16[1,16,9216]{2,1,0:T(8,128)(2,1)} %c_hbm.1), custom_call_target="tpu_custom_call" | custom-call | bytes 2500000 | tf_op jit(solution)/shard_map/pallas_call | solution.py:55
  3.3 11.0 %all-to-all-start = ((bf16[16,288,128]{2,1,0:T(8,128)(2,1)}), bf16[16,288,128]{2,1,0:T(8,128)(2,1)}, u32[]{:S(2)}, u32[]{:S(2)}) async-start(bf16[16,288,128]{2,1,0:T(8,128)(2,1)} %shard_map.58), calls=%async_computation | async-start | bytes 2359296 | tf_op jit(solution)/shard_map/all_to_all | solution.py:69
  14.3 0.0 copy-done.2
  14.3 3.3 %copy.7 = bf16[3,9,36864]{2,1,0:T(8,128)(2,1)} copy(bf16[3,9,36864]{2,0,1:T(4,128)(2,1)S(1)} %copy-done.2) | data formatting | bytes 3981312 | tf_op args[2]
  17.6 4.6 %reshape.80.w_ref = bf16[27,192,192]{2,1,0:T(8,128)(2,1)S(1)} reshape(bf16[3,9,36864]{2,1,0:T(8,128)(2,1)} %copy.7) | data formatting | bytes 3981312 | tf_op jit(solution)/shard_map/reshape | solution.py:507
  22.2 0.7 fusion.order_ref
  23.0 4.7 %all-to-all-done.recv_hbm = bf16[16,288,128]{2,1,0:T(8,128)(2,1)} async-done(((bf16[16,288,128]{2,1,0:T(8,128)(2,1)}), bf16[16,288,128]{2,1,0:T(8,128)(2,1)}, u32[]{:S(2)}, u32[]{:S(2)}) %all-to-all-start) | async-done | bytes 1179680 | tf_op jit(solution)/shard_map/all_to_all | solution.py:69
  27.7 0.0 copy-start.1
  27.7 5.4 %shard_map.59 = (bf16[3,768,192]{2,1,0:T(8,128)(2,1)S(1)}, bf16[768,192]{1,0:T(8,128)(2,1)S(1)}, bf16[768,192]{1,0:T(8,128)(2,1)S(1)}, bf16[768,192]{1,0:T(8,128...) custom-call(bf16[16,288,128]{2,1,0:T(8,128)(2,1)} %all-to-all-done.r, ...), custom_call_target="tpu_custom_call" | custom-call | flops 2038431744 | bytes 9000000 | tf_op jit(solution)/shard_map/pallas_call | solution.py:55
  33.1 0.0 copy-done.1
  33.1 2.5 %shard_map.60 = (bf16[27,144,128]{2,1,0:T(8,128)(2,1)S(1)}, bf16[27,144,128]{2,1,0:T(8,128)(2,1)S(1)}) custom-call(bf16[3,768,192]{2,1,0:T(8,128)(2,1)S(1)} %get-tuple-element.16.a0_ref, bf16[768,192]{1,0:T(8,128)(2,1)S(1)} %get-tuple-element.17.a1_ref, bf16[768,192]{1,0:T(8,128)(2,1)S(1)} %get-tuple-element.18.a2_ref, ...), custom_call_target="tpu_custom_call" | custom-call | flops 1528823808 | bytes 7000000 | tf_op jit(solution)/shard_map/pallas_call | solution.py:55
  35.6 1.9 %collective-permute-start = (bf16[27,144,128]{2,1,0:T(8,128)(2,1)S(1)}, bf16[27,144,128]{2,1,0:T(8,128)(2,1)S(1)}, u32[]{:S(2)}, u32[]{:S(2)}) collective-permute-start(bf16[27,144,128]{2,1,0:T(8,128)(2,1)S(1)} %get-tuple-element.23), channel_id=1, source_target_pairs={{0,16},{16,0},{1,17},{17,1},{2,18},{18,2},{3,19},{19,3},{4,20},{20... | collective-permute-start | bytes 2985992 | tf_op jit(solution)/shard_map/ppermute | solution.py:526
  37.5 0.8 shard_map.61.part_ref
  38.3 1.8 %collective-permute-done.got_ref = bf16[27,144,128]{2,1,0:T(8,128)(2,1)S(1)} collective-permute-done((bf16[27,144,128]{2,1,0:T(8,128)(2,1)S(1)}, bf16[27,144,128]{2,1,0:T(8,128)(2,1)S(1)}, u32[]{:S(2)}, u32[]{:S(2)}) %collective-permute-start) | collective-permute-done | bytes 995360 | tf_op jit(solution)/shard_map/ppermute | solution.py:526
  40.1 0.8 shard_map.62
  40.9 26.6 %all_to_all.15.recv_ref.got_ref = bf16[16,416,128]{2,1,0:T(8,128)(2,1)S(1)} all-to-all(bf16[16,416,128]{2,1,0:T(8,128)(2,1)S(1)} %shard_map.62), channel_id=1, replica_groups={{10,11,8,9,14,15,12,13,2,3,0,1,6,7,4,5},{26,27,24,25,30,31,28,29,18,19,..., dimensions={0} | all-to-all | bytes 3407872 | tf_op jit(solution)/shard_map/all_to_all | solution.py:69
  67.5 0.0 copy-start
  67.5 0.8 shard_map.64
  68.3 16.7 %all-to-all-start.2 = ((bf16[16,16,128]{2,1,0:T(8,128)(2,1)}), bf16[16,16,128]{2,1,0:T(8,128)(2,1)S(1)}, u32[]{:S(2)}, u32[]{:S(2)}) async-start(bf16[16,16,128]{2,1,0:T(8,128)(2,1)} %shard_map.64), calls=%async_computation.2 | async-start | bytes 131072 | tf_op jit(solution)/shard_map/all_to_all | solution.py:544
  85.0 0.0 copy-done
  85.0 2.8 %shard_map.63 = (bf16[1,16,9216]{2,1,0:T(8,128)(2,1)}, bf16[1,16,9216]{2,1,0:T(8,128)(2,1)}) custom-call(bf16[9,192,192]{2,1,0:T(8,128)(2,1)S(1)} %get-tuple-element.15.w_hbm, bf16[16,416,128]{2,1,0:T(8,128)(2,1)S(1)} %all_to_all.15.recv_ref.got_ref, bf16[1,16,9216]{2,1,0:T(8,128)(2,1)S(1)} %copy-done), custom_call_target="tpu_custom_call" | custom-call | flops 509607936 | bytes 3000000 | tf_op jit(solution)/shard_map/pallas_call | solution.py:55
  87.8 3.6 %all-to-all-done.2.refs_0_ = bf16[16,16,128]{2,1,0:T(8,128)(2,1)S(1)} async-done(((bf16[16,16,128]{2,1,0:T(8,128)(2,1)}), bf16[16,16,128]{2,1,0:T(8,128)(2,1)S(1)}, u32[]{:S(2)}, u32[]{:S(2)}) %all-to-all-start.2) | async-done | bytes 65568 | tf_op jit(solution)/shard_map/all_to_all | solution.py:544
  91.3 0.7 shard_map.65
  (1 shorter events, 0.0 us)
Async XLA Ops:
  0.6 13.7 %copy-start.2 = (bf16[3,9,36864]{2,0,1:T(4,128)(2,1)S(1)}, bf16[3,9,36864]{2,0,1:T(4,128)(2,1)}, u32[]{:S(2)}) copy-start(bf16[3,9,36864]{2,0,1:T(4,128)(2,1)} %param.5) | copy-start | bytes 5971972
  3.3 24.4 %all-to-all-start = ((bf16[16,288,128]{2,1,0:T(8,128)(2,1)}), bf16[16,288,128]{2,1,0:T(8,128)(2,1)}, u32[]{:S(2)}, u32[]{:S(2)}) async-start(bf16[16,288,128]{2,1,0:T(8,128)(2,1)} %shard_map.58), calls=%async_computation | async-start | bytes 2359296 | tf_op jit(solution)/shard_map/all_to_all | solution.py:69
  27.7 5.4 %copy-start.1 = (bf16[192,192]{1,0:T(8,128)(2,1)S(1)}, bf16[192,192]{1,0:T(8,128)(2,1)}, u32[]{:S(2)}) copy-start(bf16[192,192]{1,0:T(8,128)(2,1)} %fusion.order_ref) | copy-start | bytes 221188
  35.6 4.5 %collective-permute-start = (bf16[27,144,128]{2,1,0:T(8,128)(2,1)S(1)}, bf16[27,144,128]{2,1,0:T(8,128)(2,1)S(1)}, u32[]{:S(2)}, u32[]{:S(2)}) collective-permute-start(bf16[27,144,128]{2,1,0:T(8,128)(2,1)S(1)} %get-tuple-element.23), channel_id=1, source_target_pairs={{0,16},{16,0},{1,17},{17,1},{2,18},{18,2},{3,19},{19,3},{4,20},{20... | collective-permute-start | bytes 2985992 | tf_op jit(solution)/shard_map/ppermute | solution.py:526
  67.5 17.5 %copy-start = (bf16[1,16,9216]{2,1,0:T(8,128)(2,1)S(1)}, bf16[1,16,9216]{2,1,0:T(8,128)(2,1)}, u32[]{:S(2)}) copy-start(bf16[1,16,9216]{2,1,0:T(8,128)(2,1)} %x_ref.1) | copy-start | bytes 884740
  68.3 23.0 %all-to-all-start.2 = ((bf16[16,16,128]{2,1,0:T(8,128)(2,1)}), bf16[16,16,128]{2,1,0:T(8,128)(2,1)S(1)}, u32[]{:S(2)}, u32[]{:S(2)}) async-start(bf16[16,16,128]{2,1,0:T(8,128)(2,1)} %shard_map.64), calls=%async_computation.2 | async-start | bytes 131072 | tf_op jit(solution)/shard_map/all_to_all | solution.py:544

commit v5 on v4

--- a/solution.py
+++ b/solution.py
@@ -277,7 +277,7 @@
     first.wait()
 
 
-def final_kernel(a2_ref, s2_ref, g1_ref, w_ref, send_ref, a2p):
+def final_kernel(a2_ref, s2_ref, g1_ref, w_ref, send_ref, halo_ref, a2p):
     clear_edges(a2p, 32)
     for a in range(GROUPS):
         a2p[a, 32 : 32 + HEIGHT, :] = a2_ref[HEIGHT * a : HEIGHT * (a + 1), :]
@@ -294,20 +294,28 @@
     for k in range(3):
         both = jnp.concatenate([blocks[2 * k][:, 128:192], blocks[2 * k + 1][:, 128:192]], axis=1)
         send_ref[:, 96 + 16 * k : 112 + 16 * k, :] = both.astype(BF16).reshape(16, 16, 128)
-    third = jnp.concatenate([grads[2][:, 128:192], jnp.zeros((HEIGHT, 64), F32)], axis=1)
-    first = jnp.concatenate([grads[0][:, 128:192], grads[1][:, 128:192]], axis=1)
-    parts = [grads[0][:, 0:128], grads[1][:, 0:128], grads[2][:, 0:128], first, third]
-    index = lax.broadcasted_iota(jnp.int32, (HEIGHT, 128), 0)
-    inner = index % 16
-    halo = jnp.zeros((HEIGHT, 128), F32)
-    for n, part in enumerate(parts):
-        p = 2 * n
-        above = pltpu.roll(part, p + 1, 0)
-        halo = jnp.where((inner == p) & (index >= 16), above, halo)
-        p = 2 * n + 1
-        below = pltpu.roll(part, (HEIGHT + p - 16) % HEIGHT, 0)
-        halo = jnp.where((inner == p) & (index < HEIGHT - 16), below, halo)
-    send_ref[:, 144:160, :] = halo.astype(BF16).reshape(16, 16, 128)
+    index = lax.broadcasted_iota(jnp.int32, (HEIGHT, 64), 0)
+    wide = jnp.zeros((HEIGHT, 64), F32)
+    narrow = jnp.zeros((HEIGHT, 16), F32)
+
+    def put(total, part, row, side):
+        at = index[:, 0 : part.shape[1]]
+        if side == 0:
+            moved = pltpu.roll(part, row + 1, 0)
+            return jnp.where((at % 16 == row) & (at >= 16), moved, total)
+        moved = pltpu.roll(part, HEIGHT + row - 16, 0)
+        return jnp.where((at % 16 == row) & (at < HEIGHT - 16), moved, total)
+
+    for n in range(18):
+        a, c, side = n // 6, (n // 2) % 3, n % 2
+        part = grads[a][:, 64 * c : 64 * c + 64]
+        if n < 16:
+            wide = put(wide, part, n, side)
+            continue
+        for q in range(4):
+            narrow = put(narrow, part[:, 16 * q : 16 * q + 16], 4 * (n - 16) + q, side)
+    halo = jnp.concatenate([wide, narrow, jnp.zeros((HEIGHT, 48), F32)], axis=1)
+    halo_ref[...] = halo.astype(BF16).reshape(16, 16, 128)
 
 
 def wgrad_kernel(a0_ref, a1_ref, a2_ref, g1_ref, g2_ref, g3_ref, order_ref, keep_ref, give_ref, gp, acts):
@@ -363,9 +371,9 @@
 )
 
 
-def split_kernel(keep_ref, got_ref, part_ref, send_ref):
+def split_kernel(keep_ref, got_ref, part_ref, halo_ref, send_ref):
     for s in range(16):
-        send_ref[TURNED[s], 256:416, :] = part_ref[s]
+        send_ref[TURNED[s], 256:400, :] = part_ref[s]
 
     total = (keep_ref[...].astype(F32) + got_ref[...].astype(F32)).astype(BF16)
     for h in range(2):
@@ -381,7 +389,10 @@
                             at = 96 + 16 * j
                             first = 64 * h + max(lo, 128) - 128
                             parts.append(total[tap, at : at + 16, first : 64 * h + hi - 128])
-                parts.append(jnp.zeros((16, 80 if group == 3 else 8), BF16))
+                if group == 3:
+                    parts.append(halo_ref[8 * h + t][:, 0:80])
+                else:
+                    parts.append(jnp.zeros((16, 8), BF16))
                 line = jnp.concatenate(parts, axis=1)
                 for n in range(4):
                     at = 64 * group + 16 * n
@@ -427,7 +438,7 @@
     for k in range(3):
         both = tile(6 + k)
         highs += [both[:, 0:64], both[:, 64:128]]
-    halo = tile(9)
+    halo = slabs(recv_ref, 240).astype(F32)[:, 48:128]
     inner = lax.broadcasted_iota(jnp.int32, (HEIGHT, CH), 0) % 16
 
     def pair(left, right):
@@ -449,14 +460,20 @@
         here = jnp.concatenate([lows[a], highs[a]], axis=1)
         grads_ref[HEIGHT * a : HEIGHT * (a + 1), :] = here
 
-        def edge(row, p_lo, p_hi, lane):
-            low = pltpu.roll(halo, (row - p_lo) % HEIGHT, 0)
-            high = pltpu.roll(halo, (row - p_hi) % HEIGHT, 0)[:, lane : lane + 64]
-            return jnp.concatenate([low, high], axis=1)
-
-        hi_slot, lane = ((6, 0), (6, 64), (8, 0))[a]
-        above = edge(0, 2 * a, hi_slot, lane)
-        below = edge(15, 2 * a + 1, hi_slot + 1, lane)
+        def edge(row, side):
+            parts = []
+            for c in range(3):
+                n = 6 * a + 2 * c + side
+                if n < 16:
+                    parts.append(pltpu.roll(halo[:, 0:64], (row - n) % HEIGHT, 0))
+                    continue
+                for q in range(4):
+                    at = 4 * (n - 16) + q
+                    parts.append(pltpu.roll(halo[:, 64:80], (row - at) % HEIGHT, 0))
+            return jnp.concatenate(parts, axis=1)
+
+        above = edge(0, 0)
+        below = edge(15, 1)
         after = jnp.where(inner == 15, below, pltpu.roll(here, HEIGHT - 1, 0))
         before = jnp.where(inner == 0, above, pltpu.roll(here, 1, 0))
         padded[0, at : at + HEIGHT, :] = after.astype(BF16)
@@ -524,15 +541,15 @@
         moved=7000000,
     )
     got = lax.ppermute(give, "core", [(0, 1), (1, 0)])
-    part = call(
+    part, halo = call(
         final_kernel,
-        shape(16, 160, 128),
+        (shape(16, 144, 128), shape(16, 16, 128)),
         a2, s2, g1, kernels,
         scratch=(pltpu.VMEM((GROUPS, HEIGHT + 64, CH), BF16),),
         flops=2 * CELLS * 9 * CH * CH,
         moved=4500000,
     )
-    send = call(split_kernel, shape(16, 416, 128), keep, got, part, moved=5000000)
+    send = call(split_kernel, shape(16, 400, 128), keep, got, part, halo, moved=5000000)
     back = plane_exchange(send)
     send = call(
         gather_kernel,

time: 92.5 us -> 91.8 us (level)
  no operation moved by 1% of the time
where the time goes in v5:
time: 91.8 us; the launch traced here: 91.4 us
  starting transfers between devices  29.6 us (32%)
  blocking collectives  25.9 us (28%)
  Pallas kernels  16.6 us (18%)
  waiting for transfers between devices  9.91 us (11%)
  local copies, waits for them, and re-layouts  7.93 us (9%)
    all_to_all x1, blocking collectives, plane_exchange(): lax.all_to_all(value, 'space', 0, 0, axis_index_groups=groups, tiled=True)  25.9 us
    all_to_all x1, starting transfers between devices, body(): lax.all_to_all(send, 'z', 0, 0, axis_index_groups=[list(Z_ORDER)], tiled=...  16.7 us
    pallas_call x8, Pallas kernels, call(): pl.pallas_call(kernel, out_shape=out_shape, in_specs=[pl.BlockSpec(memory...  16.6 us
    all_to_all x1, starting transfers between devices, plane_exchange(): lax.all_to_all(value, 'space', 0, 0, axis_index_groups=groups, tiled=True)  11 us
    all_to_all x1, waiting for transfers between devices, plane_exchange(): lax.all_to_all(value, 'space', 0, 0, axis_index_groups=groups, tiled=True)  4.72 us
    reshape x1, local copies, waits for them, and re-layouts, body(): kernels = weights.reshape(27, CH, CH)  4.65 us
    all_to_all x1, waiting for transfers between devices, body(): lax.all_to_all(send, 'z', 0, 0, axis_index_groups=[list(Z_ORDER)], tiled=...  3.44 us
    unnamed x7, local copies, waits for them, and re-layouts  3.28 us
  transfers between devices with their start and end apart: 3, of which 3 were waited for; matrix products, arithmetic and copies ran while one was open for 9% of the time, Pallas kernels for 4%

profile of v5, /device:TPU:8, one launch (start us, length us, event | category | flops | bytes accessed | tf_op | source)
XLA Modules:
  0.0 91.4 jit_solution(7104724899494851068)
XLA Ops:
  0.6 0.0 copy-start.2
  0.6 2.7 %shard_map.58 = bf16[16,288,128]{2,1,0:T(8,128)(2,1)} custom-call(bf16[1,16,9216]{2,1,0:T(8,128)(2,1)} %x_ref.1, bf16[1,16,9216]{2,1,0:T(8,128)(2,1)} %c_hbm.1), custom_call_target="tpu_custom_call" | custom-call | bytes 2500000 | tf_op jit(solution)/shard_map/pallas_call | solution.py:55
  3.3 11.0 %all-to-all-start = ((bf16[16,288,128]{2,1,0:T(8,128)(2,1)}), bf16[16,288,128]{2,1,0:T(8,128)(2,1)}, u32[]{:S(2)}, u32[]{:S(2)}) async-start(bf16[16,288,128]{2,1,0:T(8,128)(2,1)} %shard_map.58), calls=%async_computation | async-start | bytes 2359296 | tf_op jit(solution)/shard_map/all_to_all | solution.py:69
  14.3 0.0 copy-done.2
  14.3 3.3 %copy.7 = bf16[3,9,36864]{2,1,0:T(8,128)(2,1)} copy(bf16[3,9,36864]{2,0,1:T(4,128)(2,1)S(1)} %copy-done.2) | data formatting | bytes 3981312 | tf_op args[2]
  17.6 4.6 %reshape.80.w_ref = bf16[27,192,192]{2,1,0:T(8,128)(2,1)S(1)} reshape(bf16[3,9,36864]{2,1,0:T(8,128)(2,1)} %copy.7) | data formatting | bytes 3981312 | tf_op jit(solution)/shard_map/reshape | solution.py:524
  22.3 0.7 fusion.order_ref
  23.0 4.7 %all-to-all-done.recv_hbm = bf16[16,288,128]{2,1,0:T(8,128)(2,1)} async-done(((bf16[16,288,128]{2,1,0:T(8,128)(2,1)}), bf16[16,288,128]{2,1,0:T(8,128)(2,1)}, u32[]{:S(2)}, u32[]{:S(2)}) %all-to-all-start) | async-done | bytes 1179680 | tf_op jit(solution)/shard_map/all_to_all | solution.py:69
  27.7 0.0 copy-start.1
  27.7 5.4 %shard_map.59 = (bf16[3,768,192]{2,1,0:T(8,128)(2,1)S(1)}, bf16[768,192]{1,0:T(8,128)(2,1)S(1)}, bf16[768,192]{1,0:T(8,128)(2,1)S(1)}, bf16[768,192]{1,0:T(8,128...) custom-call(bf16[16,288,128]{2,1,0:T(8,128)(2,1)} %all-to-all-done.r, ...), custom_call_target="tpu_custom_call" | custom-call | flops 2038431744 | bytes 9000000 | tf_op jit(solution)/shard_map/pallas_call | solution.py:55
  33.1 0.0 copy-done.1
  33.1 2.5 %shard_map.60 = (bf16[27,144,128]{2,1,0:T(8,128)(2,1)S(1)}, bf16[27,144,128]{2,1,0:T(8,128)(2,1)S(1)}) custom-call(bf16[3,768,192]{2,1,0:T(8,128)(2,1)S(1)} %get-tuple-element.18.a0_ref, bf16[768,192]{1,0:T(8,128)(2,1)S(1)} %get-tuple-element.19.a1_ref, bf16[768,192]{1,0:T(8,128)(2,1)S(1)} %get-tuple-element.20.a2_ref, ...), custom_call_target="tpu_custom_call" | custom-call | flops 1528823808 | bytes 7000000 | tf_op jit(solution)/shard_map/pallas_call | solution.py:55
  35.6 1.9 %collective-permute-start = (bf16[27,144,128]{2,1,0:T(8,128)(2,1)S(1)}, bf16[27,144,128]{2,1,0:T(8,128)(2,1)S(1)}, u32[]{:S(2)}, u32[]{:S(2)}) collective-permute-start(bf16[27,144,128]{2,1,0:T(8,128)(2,1)S(1)} %get-tuple-element.25), channel_id=1, source_target_pairs={{0,16},{16,0},{1,17},{17,1},{2,18},{18,2},{3,19},{19,3},{4,20},{20... | collective-permute-start | bytes 2985992 | tf_op jit(solution)/shard_map/ppermute | solution.py:543
  37.6 0.8 shard_map.61
  38.4 1.8 %collective-permute-done.got_ref = bf16[27,144,128]{2,1,0:T(8,128)(2,1)S(1)} collective-permute-done((bf16[27,144,128]{2,1,0:T(8,128)(2,1)S(1)}, bf16[27,144,128]{2,1,0:T(8,128)(2,1)S(1)}, u32[]{:S(2)}, u32[]{:S(2)}) %collective-permute-start) | collective-permute-done | bytes 995360 | tf_op jit(solution)/shard_map/ppermute | solution.py:543
  40.1 0.8 shard_map.62
  40.9 25.9 %all_to_all.15.recv_ref.got_ref = bf16[16,400,128]{2,1,0:T(8,128)(2,1)S(1)} all-to-all(bf16[16,400,128]{2,1,0:T(8,128)(2,1)S(1)} %shard_map.62), channel_id=1, replica_groups={{10,11,8,9,14,15,12,13,2,3,0,1,6,7,4,5},{26,27,24,25,30,31,28,29,18,19,..., dimensions={0} | all-to-all | bytes 3276800 | tf_op jit(solution)/shard_map/all_to_all | solution.py:69
  66.8 0.0 copy-start
  66.8 0.8 shard_map.64
  67.6 16.7 %all-to-all-start.2 = ((bf16[16,16,128]{2,1,0:T(8,128)(2,1)}), bf16[16,16,128]{2,1,0:T(8,128)(2,1)S(1)}, u32[]{:S(2)}, u32[]{:S(2)}) async-start(bf16[16,16,128]{2,1,0:T(8,128)(2,1)} %shard_map.64), calls=%async_computation.2 | async-start | bytes 131072 | tf_op jit(solution)/shard_map/all_to_all | solution.py:561
  84.3 0.0 copy-done
  84.3 2.9 %shard_map.63 = (bf16[1,16,9216]{2,1,0:T(8,128)(2,1)}, bf16[1,16,9216]{2,1,0:T(8,128)(2,1)}) custom-call(bf16[9,192,192]{2,1,0:T(8,128)(2,1)S(1)} %get-tuple-element.17.w_hbm, bf16[16,400,128]{2,1,0:T(8,128)(2,1)S(1)} %all_to_all.15.recv_ref.got_ref, bf16[1,16,9216]{2,1,0:T(8,128)(2,1)S(1)} %copy-done), custom_call_target="tpu_custom_call" | custom-call | flops 509607936 | bytes 3000000 | tf_op jit(solution)/shard_map/pallas_call | solution.py:55
  87.2 3.4 %all-to-all-done.2.refs_0_ = bf16[16,16,128]{2,1,0:T(8,128)(2,1)S(1)} async-done(((bf16[16,16,128]{2,1,0:T(8,128)(2,1)}), bf16[16,16,128]{2,1,0:T(8,128)(2,1)S(1)}, u32[]{:S(2)}, u32[]{:S(2)}) %all-to-all-start.2) | async-done | bytes 65568 | tf_op jit(solution)/shard_map/all_to_all | solution.py:561
  90.7 0.7 shard_map.65
  (1 shorter events, 0.0 us)
Async XLA Ops:
  0.6 13.7 %copy-start.2 = (bf16[3,9,36864]{2,0,1:T(4,128)(2,1)S(1)}, bf16[3,9,36864]{2,0,1:T(4,128)(2,1)}, u32[]{:S(2)}) copy-start(bf16[3,9,36864]{2,0,1:T(4,128)(2,1)} %param.5) | copy-start | bytes 5971972
  3.3 24.4 %all-to-all-start = ((bf16[16,288,128]{2,1,0:T(8,128)(2,1)}), bf16[16,288,128]{2,1,0:T(8,128)(2,1)}, u32[]{:S(2)}, u32[]{:S(2)}) async-start(bf16[16,288,128]{2,1,0:T(8,128)(2,1)} %shard_map.58), calls=%async_computation | async-start | bytes 2359296 | tf_op jit(solution)/shard_map/all_to_all | solution.py:69
  27.7 5.4 %copy-start.1 = (bf16[192,192]{1,0:T(8,128)(2,1)S(1)}, bf16[192,192]{1,0:T(8,128)(2,1)}, u32[]{:S(2)}) copy-start(bf16[192,192]{1,0:T(8,128)(2,1)} %fusion.order_ref) | copy-start | bytes 221188
  35.6 4.5 %collective-permute-start = (bf16[27,144,128]{2,1,0:T(8,128)(2,1)S(1)}, bf16[27,144,128]{2,1,0:T(8,128)(2,1)S(1)}, u32[]{:S(2)}, u32[]{:S(2)}) collective-permute-start(bf16[27,144,128]{2,1,0:T(8,128)(2,1)S(1)} %get-tuple-element.25), channel_id=1, source_target_pairs={{0,16},{16,0},{1,17},{17,1},{2,18},{18,2},{3,19},{19,3},{4,20},{20... | collective-permute-start | bytes 2985992 | tf_op jit(solution)/shard_map/ppermute | solution.py:543
  66.8 17.5 %copy-start = (bf16[1,16,9216]{2,1,0:T(8,128)(2,1)S(1)}, bf16[1,16,9216]{2,1,0:T(8,128)(2,1)}, u32[]{:S(2)}) copy-start(bf16[1,16,9216]{2,1,0:T(8,128)(2,1)} %x_ref.1) | copy-start | bytes 884740
  67.6 23.0 %all-to-all-start.2 = ((bf16[16,16,128]{2,1,0:T(8,128)(2,1)}), bf16[16,16,128]{2,1,0:T(8,128)(2,1)S(1)}, u32[]{:S(2)}, u32[]{:S(2)}) async-start(bf16[16,16,128]{2,1,0:T(8,128)(2,1)} %shard_map.64), calls=%async_computation.2 | async-start | bytes 131072 | tf_op jit(solution)/shard_map/all_to_all | solution.py:561

commit v6 on v5

--- a/solution.py
+++ b/solution.py
@@ -177,12 +177,12 @@
     pltpu.VMEM((GROUPS, HEIGHT + 64, CH), BF16),
     pltpu.VMEM((CELLS, CH), F32),
     pltpu.VMEM((CELLS, CH), F32),
-    pltpu.SemaphoreType.DMA((4,)),
+    pltpu.SemaphoreType.DMA((3,)),
 )
 
 
 def main_kernel(
-    recv_hbm, w_ref, a0_ref, a1_ref, a2_ref, g1_ref, g2_ref, g3_ref, s2_ref, first_hbm,
+    recv_hbm, w_ref, a0_ref, a1_ref, a2_ref, g1_ref, g2_ref, g3_ref, s2_ref,
     recv_ref, a0p, a1p, g2p, g3p, slope1, slope2, sems,
 ):
     def rows_copy(n, lo, hi):
@@ -192,7 +192,6 @@
         part.start()
         return part
 
-    first = pltpu.make_async_copy(w_ref.at[0:9], first_hbm, sems.at[3])
     moving = [rows_copy(0, 0, 144), rows_copy(1, 192, 288), rows_copy(2, 144, 192)]
 
     def block(k):
@@ -203,7 +202,6 @@
     for ref, pad in ((a1p, 16), (g2p, 16), (g3p, 32)):
         clear_edges(ref, pad)
 
-    first.start()
     moving[0].wait()
     moving[1].wait()
     state = []
@@ -274,10 +272,11 @@
     near2 = spread_conv_at(2, *near)
     third_grad(1, near1)
     third_grad(2, near2)
-    first.wait()
-
-
-def final_kernel(a2_ref, s2_ref, g1_ref, w_ref, send_ref, halo_ref, a2p):
+
+
+def final_kernel(a2_ref, s2_ref, g1_ref, w_ref, send_ref, halo_ref, first_hbm, a2p, sem):
+    first = pltpu.make_async_copy(w_ref.at[0:9], first_hbm, sem)
+    first.start()
     clear_edges(a2p, 32)
     for a in range(GROUPS):
         a2p[a, 32 : 32 + HEIGHT, :] = a2_ref[HEIGHT * a : HEIGHT * (a + 1), :]
@@ -316,6 +315,7 @@
             narrow = put(narrow, part[:, 16 * q : 16 * q + 16], 4 * (n - 16) + q, side)
     halo = jnp.concatenate([wide, narrow, jnp.zeros((HEIGHT, 48), F32)], axis=1)
     halo_ref[...] = halo.astype(BF16).reshape(16, 16, 128)
+    first.wait()
 
 
 def wgrad_kernel(a0_ref, a1_ref, a2_ref, g1_ref, g2_ref, g3_ref, order_ref, keep_ref, give_ref, gp, acts):
@@ -522,13 +522,12 @@
     )
     recv = plane_exchange(send)
     kernels = weights.reshape(27, CH, CH)
-    a0, a1, a2, g1, g2, g3, s2, first = call(
+    a0, a1, a2, g1, g2, g3, s2 = call(
         main_kernel,
-        (shape(3, CELLS, CH),) + (shape(CELLS, CH),) * 6 + (shape(9, CH, CH),),
+        (shape(3, CELLS, CH),) + (shape(CELLS, CH),) * 6,
         kernels,
         remain=(recv,),
         scratch=MAIN_SCRATCH,
-        apart=1,
         flops=4 * 2 * CELLS * 9 * CH * CH,
         moved=9000000,
     )
@@ -541,13 +540,14 @@
         moved=7000000,
     )
     got = lax.ppermute(give, "core", [(0, 1), (1, 0)])
-    part, halo = call(
+    part, halo, first = call(
         final_kernel,
-        (shape(16, 144, 128), shape(16, 16, 128)),
+        (shape(16, 144, 128), shape(16, 16, 128), shape(9, CH, CH)),
         a2, s2, g1, kernels,
-        scratch=(pltpu.VMEM((GROUPS, HEIGHT + 64, CH), BF16),),
+        scratch=(pltpu.VMEM((GROUPS, HEIGHT + 64, CH), BF16), pltpu.SemaphoreType.DMA),
         flops=2 * CELLS * 9 * CH * CH,
         moved=4500000,
+        apart=1,
     )
     send = call(split_kernel, shape(16, 400, 128), keep, got, part, halo, moved=5000000)
     back = plane_exchange(send)

time: 91.8 us -> 91.7 us (level)
    unnamed x7 -> x5, local copies, waits for them, and re-layouts: 3.28 us -> 3.28 us
where the time goes in v6:
time: 91.7 us; the launch traced here: 91.3 us
  starting transfers between devices  29.6 us (32%)
  blocking collectives  25.9 us (28%)
  Pallas kernels  16.7 us (18%)
  waiting for transfers between devices  10.3 us (11%)
  local copies, waits for them, and re-layouts  7.93 us (9%)
    all_to_all x1, blocking collectives, plane_exchange(): lax.all_to_all(value, 'space', 0, 0, axis_index_groups=groups, tiled=True)  25.9 us
    pallas_call x8, Pallas kernels, call(): pl.pallas_call(kernel, out_shape=out_shape, in_specs=[pl.BlockSpec(memory...  16.7 us
    all_to_all x1, starting transfers between devices, body(): lax.all_to_all(send, 'z', 0, 0, axis_index_groups=[list(Z_ORDER)], tiled=...  16.7 us
    all_to_all x1, starting transfers between devices, plane_exchange(): lax.all_to_all(value, 'space', 0, 0, axis_index_groups=groups, tiled=True)  11 us
    all_to_all x1, waiting for transfers between devices, plane_exchange(): lax.all_to_all(value, 'space', 0, 0, axis_index_groups=groups, tiled=True)  5.34 us
    reshape x1, local copies, waits for them, and re-layouts, body(): kernels = weights.reshape(27, CH, CH)  4.65 us
    all_to_all x1, waiting for transfers between devices, body(): lax.all_to_all(send, 'z', 0, 0, axis_index_groups=[list(Z_ORDER)], tiled=...  3.44 us
    unnamed x5, local copies, waits for them, and re-layouts  3.28 us
  transfers between devices with their start and end apart: 3, of which 3 were waited for; matrix products, arithmetic and copies ran while one was open for 9% of the time, Pallas kernels for 4%

profile of v6, /device:TPU:8, one launch (start us, length us, event | category | flops | bytes accessed | tf_op | source)
XLA Modules:
  0.0 91.3 jit_solution(3944795302248380522)
XLA Ops:
  0.6 0.0 copy-start.1
  0.6 2.6 %shard_map.58 = bf16[16,288,128]{2,1,0:T(8,128)(2,1)} custom-call(bf16[1,16,9216]{2,1,0:T(8,128)(2,1)} %x_ref.1, bf16[1,16,9216]{2,1,0:T(8,128)(2,1)} %c_hbm.1), custom_call_target="tpu_custom_call" | custom-call | bytes 2500000 | tf_op jit(solution)/shard_map/pallas_call | solution.py:55
  3.3 11.0 %all-to-all-start = ((bf16[16,288,128]{2,1,0:T(8,128)(2,1)}), bf16[16,288,128]{2,1,0:T(8,128)(2,1)}, u32[]{:S(2)}, u32[]{:S(2)}) async-start(bf16[16,288,128]{2,1,0:T(8,128)(2,1)} %shard_map.58), calls=%async_computation | async-start | bytes 2359296 | tf_op jit(solution)/shard_map/all_to_all | solution.py:69
  14.3 0.0 copy-done.1
  14.3 3.3 %copy.7 = bf16[3,9,36864]{2,1,0:T(8,128)(2,1)} copy(bf16[3,9,36864]{2,0,1:T(4,128)(2,1)S(1)} %copy-done.1) | data formatting | bytes 3981312 | tf_op args[2]
  17.6 4.6 %reshape.80.w_ref = bf16[27,192,192]{2,1,0:T(8,128)(2,1)S(1)} reshape(bf16[3,9,36864]{2,1,0:T(8,128)(2,1)} %copy.7) | data formatting | bytes 3981312 | tf_op jit(solution)/shard_map/reshape | solution.py:524
  22.2 0.1 fusion.order_ref
  22.3 5.3 %all-to-all-done.recv_hbm = bf16[16,288,128]{2,1,0:T(8,128)(2,1)} async-done(((bf16[16,288,128]{2,1,0:T(8,128)(2,1)}), bf16[16,288,128]{2,1,0:T(8,128)(2,1)}, u32[]{:S(2)}, u32[]{:S(2)}) %all-to-all-start) | async-done | bytes 1179680 | tf_op jit(solution)/shard_map/all_to_all | solution.py:69
  27.7 5.3 %shard_map.59 = (bf16[3,768,192]{2,1,0:T(8,128)(2,1)S(1)}, bf16[768,192]{1,0:T(8,128)(2,1)S(1)}, bf16[768,192]{1,0:T(8,128)(2,1)S(1)}, bf16[768,192]{1,0:T(8,128...) custom-call(bf16[16,288,128]{2,1,0:T(8,128)(2,1)} %all-to-all-done.recv_hbm, ...), custom_call_target="tpu_custom_call" | custom-call | flops 2038431744 | bytes 9000000 | tf_op jit(solution)/shard_map/pallas_call | solution.py:55
  33.0 2.5 %shard_map.61 = (bf16[27,144,128]{2,1,0:T(8,128)(2,1)S(1)}, bf16[27,144,128]{2,1,0:T(8,128)(2,1)S(1)}) custom-call(bf16[3,768,192]{2,1,0:T(8,128)(2,1)S(1)} %get-tuple-element.21.a0_ref, bf16[768,192]{1,0:T(8,128)(2,1)S(1)} %get-tuple-element.22.a1_ref, bf16[768,192]{1,0:T(8,128)(2,1)S(1)} %get-tuple-element.17.a2_ref, ...), custom_call_target="tpu_custom_call" | custom-call | flops 1528823808 | bytes 7000000 | tf_op jit(solution)/shard_map/pallas_call | solution.py:55
  35.6 1.9 %collective-permute-start = (bf16[27,144,128]{2,1,0:T(8,128)(2,1)S(1)}, bf16[27,144,128]{2,1,0:T(8,128)(2,1)S(1)}, u32[]{:S(2)}, u32[]{:S(2)}) collective-permute-start(bf16[27,144,128]{2,1,0:T(8,128)(2,1)S(1)} %get-tuple-element.26), channel_id=1, source_target_pairs={{0,16},{16,0},{1,17},{17,1},{2,18},{18,2},{3,19},{19,3},{4,20},{20... | collective-permute-start | bytes 2985992 | tf_op jit(solution)/shard_map/ppermute | solution.py:542
  37.5 1.0 %shard_map.60 = (bf16[16,144,128]{2,1,0:T(8,128)(2,1)S(1)}, bf16[16,16,128]{2,1,0:T(8,128)(2,1)S(1)}, bf16[9,192,192]{2,1,0:T(8,128)(2,1)S(1)}) custom-call(bf16[768,192]{1,0:T(8,128)(2,1)S(1)} %get-tuple-element.17.a2_ref, bf16[768,192]{1,0:T(8,128)(2,1)S(1)} %get-tuple-element.18.s2_ref, bf16[768,192]{1,0:T(8,128)(2,1)S(1)} %get-tuple-element.19.g1_ref, ...), custom_call_target="tpu_custom_call" | custom-call | flops 509607936 | bytes 4500000 | tf_op jit(solution)/shard_map/pallas_call | solution.py:55
  38.5 1.5 %collective-permute-done.got_ref = bf16[27,144,128]{2,1,0:T(8,128)(2,1)S(1)} collective-permute-done((bf16[27,144,128]{2,1,0:T(8,128)(2,1)S(1)}, bf16[27,144,128]{2,1,0:T(8,128)(2,1)S(1)}, u32[]{:S(2)}, u32[]{:S(2)}) %collective-permute-start) | collective-permute-done | bytes 995360 | tf_op jit(solution)/shard_map/ppermute | solution.py:542
  40.0 0.8 shard_map.62
  40.8 25.9 %all_to_all.15.recv_ref.got_ref = bf16[16,400,128]{2,1,0:T(8,128)(2,1)S(1)} all-to-all(bf16[16,400,128]{2,1,0:T(8,128)(2,1)S(1)} %shard_map.62), channel_id=1, replica_groups={{10,11,8,9,14,15,12,13,2,3,0,1,6,7,4,5},{26,27,24,25,30,31,28,29,18,19,..., dimensions={0} | all-to-all | bytes 3276800 | tf_op jit(solution)/shard_map/all_to_all | solution.py:69
  66.7 0.0 copy-start
  66.8 0.8 shard_map.64
  67.6 16.7 %all-to-all-start.2 = ((bf16[16,16,128]{2,1,0:T(8,128)(2,1)}), bf16[16,16,128]{2,1,0:T(8,128)(2,1)S(1)}, u32[]{:S(2)}, u32[]{:S(2)}) async-start(bf16[16,16,128]{2,1,0:T(8,128)(2,1)} %shard_map.64), calls=%async_computation.2 | async-start | bytes 131072 | tf_op jit(solution)/shard_map/all_to_all | solution.py:561
  84.3 0.0 copy-done
  84.3 2.9 %shard_map.63 = (bf16[1,16,9216]{2,1,0:T(8,128)(2,1)}, bf16[1,16,9216]{2,1,0:T(8,128)(2,1)}) custom-call(bf16[9,192,192]{2,1,0:T(8,128)(2,1)S(1)} %get-tuple-element.20.w_hbm, bf16[16,400,128]{2,1,0:T(8,128)(2,1)S(1)} %all_to_all.15.recv_ref.got_ref, bf16[1,16,9216]{2,1,0:T(8,128)(2,1)S(1)} %copy-done), custom_call_target="tpu_custom_call" | custom-call | flops 509607936 | bytes 3000000 | tf_op jit(solution)/shard_map/pallas_call | solution.py:55
  87.2 3.4 %all-to-all-done.2.refs_0_ = bf16[16,16,128]{2,1,0:T(8,128)(2,1)S(1)} async-done(((bf16[16,16,128]{2,1,0:T(8,128)(2,1)}), bf16[16,16,128]{2,1,0:T(8,128)(2,1)S(1)}, u32[]{:S(2)}, u32[]{:S(2)}) %all-to-all-start.2) | async-done | bytes 65568 | tf_op jit(solution)/shard_map/all_to_all | solution.py:561
  90.6 0.7 shard_map.65
  (1 shorter events, 0.0 us)
Async XLA Ops:
  0.6 13.7 %copy-start.1 = (bf16[3,9,36864]{2,0,1:T(4,128)(2,1)S(1)}, bf16[3,9,36864]{2,0,1:T(4,128)(2,1)}, u32[]{:S(2)}) copy-start(bf16[3,9,36864]{2,0,1:T(4,128)(2,1)} %param.5) | copy-start | bytes 5971972
  3.3 24.4 %all-to-all-start = ((bf16[16,288,128]{2,1,0:T(8,128)(2,1)}), bf16[16,288,128]{2,1,0:T(8,128)(2,1)}, u32[]{:S(2)}, u32[]{:S(2)}) async-start(bf16[16,288,128]{2,1,0:T(8,128)(2,1)} %shard_map.58), calls=%async_computation | async-start | bytes 2359296 | tf_op jit(solution)/shard_map/all_to_all | solution.py:69
  35.6 4.5 %collective-permute-start = (bf16[27,144,128]{2,1,0:T(8,128)(2,1)S(1)}, bf16[27,144,128]{2,1,0:T(8,128)(2,1)S(1)}, u32[]{:S(2)}, u32[]{:S(2)}) collective-permute-start(bf16[27,144,128]{2,1,0:T(8,128)(2,1)S(1)} %get-tuple-element.26), channel_id=1, source_target_pairs={{0,16},{16,0},{1,17},{17,1},{2,18},{18,2},{3,19},{19,3},{4,20},{20... | collective-permute-start | bytes 2985992 | tf_op jit(solution)/shard_map/ppermute | solution.py:542
  66.7 17.5 %copy-start = (bf16[1,16,9216]{2,1,0:T(8,128)(2,1)S(1)}, bf16[1,16,9216]{2,1,0:T(8,128)(2,1)}, u32[]{:S(2)}) copy-start(bf16[1,16,9216]{2,1,0:T(8,128)(2,1)} %x_ref.1) | copy-start | bytes 884740
  67.6 23.0 %all-to-all-start.2 = ((bf16[16,16,128]{2,1,0:T(8,128)(2,1)}), bf16[16,16,128]{2,1,0:T(8,128)(2,1)S(1)}, u32[]{:S(2)}, u32[]{:S(2)}) async-start(bf16[16,16,128]{2,1,0:T(8,128)(2,1)} %shard_map.64), calls=%async_computation.2 | async-start | bytes 131072 | tf_op jit(solution)/shard_map/all_to_all | solution.py:561

commit v7 on v6

--- a/solution.py
+++ b/solution.py
@@ -192,7 +192,7 @@
         part.start()
         return part
 
-    moving = [rows_copy(0, 0, 144), rows_copy(1, 192, 288), rows_copy(2, 144, 192)]
+    moving = [rows_copy(0, 0, 144), rows_copy(1, 192, 288)]
 
     def block(k):
         lo = slabs(recv_ref, 16 * k)
@@ -204,6 +204,7 @@
 
     moving[0].wait()
     moving[1].wait()
+    moving.append(rows_copy(2, 144, 192))
     state = []
     for a in range(GROUPS):
         rows = slice(HEIGHT * a, HEIGHT * (a + 1))

time: 91.7 us -> 91.7 us (level)
  no operation moved by 1% of the time
where the time goes in v7:
time: 91.7 us; the launch traced here: 91.3 us
  starting transfers between devices  29.6 us (32%)
  blocking collectives  25.9 us (28%)
  Pallas kernels  16.7 us (18%)
  waiting for transfers between devices  10.3 us (11%)
  local copies, waits for them, and re-layouts  7.93 us (9%)
    all_to_all x1, blocking collectives, plane_exchange(): lax.all_to_all(value, 'space', 0, 0, axis_index_groups=groups, tiled=True)  25.9 us
    pallas_call x8, Pallas kernels, call(): pl.pallas_call(kernel, out_shape=out_shape, in_specs=[pl.BlockSpec(memory...  16.7 us
    all_to_all x1, starting transfers between devices, body(): lax.all_to_all(send, 'z', 0, 0, axis_index_groups=[list(Z_ORDER)], tiled=...  16.7 us
    all_to_all x1, starting transfers between devices, plane_exchange(): lax.all_to_all(value, 'space', 0, 0, axis_index_groups=groups, tiled=True)  11 us
    all_to_all x1, waiting for transfers between devices, plane_exchange(): lax.all_to_all(value, 'space', 0, 0, axis_index_groups=groups, tiled=True)  5.34 us
    reshape x1, local copies, waits for them, and re-layouts, body(): kernels = weights.reshape(27, CH, CH)  4.65 us
    all_to_all x1, waiting for transfers between devices, body(): lax.all_to_all(send, 'z', 0, 0, axis_index_groups=[list(Z_ORDER)], tiled=...  3.44 us
    unnamed x5, local copies, waits for them, and re-layouts  3.28 us
  transfers between devices with their start and end apart: 3, of which 3 were waited for; matrix products, arithmetic and copies ran while one was open for 9% of the time, Pallas kernels for 4%

profile of v7, /device:TPU:8, one launch (start us, length us, event | category | flops | bytes accessed | tf_op | source)
XLA Modules:
  0.0 91.3 jit_solution(10320888307981877829)
XLA Ops:
  0.6 0.0 copy-start.1
  0.6 2.6 %shard_map.58 = bf16[16,288,128]{2,1,0:T(8,128)(2,1)} custom-call(bf16[1,16,9216]{2,1,0:T(8,128)(2,1)} %x_ref.1, bf16[1,16,9216]{2,1,0:T(8,128)(2,1)} %c_hbm.1), custom_call_target="tpu_custom_call" | custom-call | bytes 2500000 | tf_op jit(solution)/shard_map/pallas_call | solution.py:55
  3.3 11.0 %all-to-all-start = ((bf16[16,288,128]{2,1,0:T(8,128)(2,1)}), bf16[16,288,128]{2,1,0:T(8,128)(2,1)}, u32[]{:S(2)}, u32[]{:S(2)}) async-start(bf16[16,288,128]{2,1,0:T(8,128)(2,1)} %shard_map.58), calls=%async_computation | async-start | bytes 2359296 | tf_op jit(solution)/shard_map/all_to_all | solution.py:69
  14.3 0.0 copy-done.1
  14.3 3.3 %copy.7 = bf16[3,9,36864]{2,1,0:T(8,128)(2,1)} copy(bf16[3,9,36864]{2,0,1:T(4,128)(2,1)S(1)} %copy-done.1) | data formatting | bytes 3981312 | tf_op args[2]
  17.6 4.6 %reshape.80.w_ref = bf16[27,192,192]{2,1,0:T(8,128)(2,1)S(1)} reshape(bf16[3,9,36864]{2,1,0:T(8,128)(2,1)} %copy.7) | data formatting | bytes 3981312 | tf_op jit(solution)/shard_map/reshape | solution.py:525
  22.2 0.1 fusion.order_ref
  22.3 5.3 %all-to-all-done.recv_hbm = bf16[16,288,128]{2,1,0:T(8,128)(2,1)} async-done(((bf16[16,288,128]{2,1,0:T(8,128)(2,1)}), bf16[16,288,128]{2,1,0:T(8,128)(2,1)}, u32[]{:S(2)}, u32[]{:S(2)}) %all-to-all-start) | async-done | bytes 1179680 | tf_op jit(solution)/shard_map/all_to_all | solution.py:69
  27.7 5.3 %shard_map.59 = (bf16[3,768,192]{2,1,0:T(8,128)(2,1)S(1)}, bf16[768,192]{1,0:T(8,128)(2,1)S(1)}, bf16[768,192]{1,0:T(8,128)(2,1)S(1)}, bf16[768,192]{1,0:T(8,128...) custom-call(bf16[16,288,128]{2,1,0:T(8,128)(2,1)} %all-to-all-done.recv_hbm, ...), custom_call_target="tpu_custom_call" | custom-call | flops 2038431744 | bytes 9000000 | tf_op jit(solution)/shard_map/pallas_call | solution.py:55
  33.0 2.5 %shard_map.61 = (bf16[27,144,128]{2,1,0:T(8,128)(2,1)S(1)}, bf16[27,144,128]{2,1,0:T(8,128)(2,1)S(1)}) custom-call(bf16[3,768,192]{2,1,0:T(8,128)(2,1)S(1)} %get-tuple-element.21.a0_ref, bf16[768,192]{1,0:T(8,128)(2,1)S(1)} %get-tuple-element.22.a1_ref, bf16[768,192]{1,0:T(8,128)(2,1)S(1)} %get-tuple-element.17.a2_ref, ...), custom_call_target="tpu_custom_call" | custom-call | flops 1528823808 | bytes 7000000 | tf_op jit(solution)/shard_map/pallas_call | solution.py:55
  35.6 1.9 %collective-permute-start = (bf16[27,144,128]{2,1,0:T(8,128)(2,1)S(1)}, bf16[27,144,128]{2,1,0:T(8,128)(2,1)S(1)}, u32[]{:S(2)}, u32[]{:S(2)}) collective-permute-start(bf16[27,144,128]{2,1,0:T(8,128)(2,1)S(1)} %get-tuple-element.26), channel_id=1, source_target_pairs={{0,16},{16,0},{1,17},{17,1},{2,18},{18,2},{3,19},{19,3},{4,20},{20... | collective-permute-start | bytes 2985992 | tf_op jit(solution)/shard_map/ppermute | solution.py:543
  37.5 1.0 %shard_map.60 = (bf16[16,144,128]{2,1,0:T(8,128)(2,1)S(1)}, bf16[16,16,128]{2,1,0:T(8,128)(2,1)S(1)}, bf16[9,192,192]{2,1,0:T(8,128)(2,1)S(1)}) custom-call(bf16[768,192]{1,0:T(8,128)(2,1)S(1)} %get-tuple-element.17.a2_ref, bf16[768,192]{1,0:T(8,128)(2,1)S(1)} %get-tuple-element.18.s2_ref, bf16[768,192]{1,0:T(8,128)(2,1)S(1)} %get-tuple-element.19.g1_ref, ...), custom_call_target="tpu_custom_call" | custom-call | flops 509607936 | bytes 4500000 | tf_op jit(solution)/shard_map/pallas_call | solution.py:55
  38.5 1.5 %collective-permute-done.got_ref = bf16[27,144,128]{2,1,0:T(8,128)(2,1)S(1)} collective-permute-done((bf16[27,144,128]{2,1,0:T(8,128)(2,1)S(1)}, bf16[27,144,128]{2,1,0:T(8,128)(2,1)S(1)}, u32[]{:S(2)}, u32[]{:S(2)}) %collective-permute-start) | collective-permute-done | bytes 995360 | tf_op jit(solution)/shard_map/ppermute | solution.py:543
  40.0 0.8 shard_map.62
  40.8 25.9 %all_to_all.15.recv_ref.got_ref = bf16[16,400,128]{2,1,0:T(8,128)(2,1)S(1)} all-to-all(bf16[16,400,128]{2,1,0:T(8,128)(2,1)S(1)} %shard_map.62), channel_id=1, replica_groups={{10,11,8,9,14,15,12,13,2,3,0,1,6,7,4,5},{26,27,24,25,30,31,28,29,18,19,..., dimensions={0} | all-to-all | bytes 3276800 | tf_op jit(solution)/shard_map/all_to_all | solution.py:69
  66.8 0.0 copy-start
  66.8 0.8 shard_map.64
  67.6 16.7 %all-to-all-start.2 = ((bf16[16,16,128]{2,1,0:T(8,128)(2,1)}), bf16[16,16,128]{2,1,0:T(8,128)(2,1)S(1)}, u32[]{:S(2)}, u32[]{:S(2)}) async-start(bf16[16,16,128]{2,1,0:T(8,128)(2,1)} %shard_map.64), calls=%async_computation.2 | async-start | bytes 131072 | tf_op jit(solution)/shard_map/all_to_all | solution.py:562
  84.2 0.0 copy-done
  84.2 2.9 %shard_map.63 = (bf16[1,16,9216]{2,1,0:T(8,128)(2,1)}, bf16[1,16,9216]{2,1,0:T(8,128)(2,1)}) custom-call(bf16[9,192,192]{2,1,0:T(8,128)(2,1)S(1)} %get-tuple-element.20.w_hbm, bf16[16,400,128]{2,1,0:T(8,128)(2,1)S(1)} %all_to_all.15.recv_ref.got_ref, bf16[1,16,9216]{2,1,0:T(8,128)(2,1)S(1)} %copy-done), custom_call_target="tpu_custom_call" | custom-call | flops 509607936 | bytes 3000000 | tf_op jit(solution)/shard_map/pallas_call | solution.py:55
  87.2 3.4 %all-to-all-done.2.refs_0_ = bf16[16,16,128]{2,1,0:T(8,128)(2,1)S(1)} async-done(((bf16[16,16,128]{2,1,0:T(8,128)(2,1)}), bf16[16,16,128]{2,1,0:T(8,128)(2,1)S(1)}, u32[]{:S(2)}, u32[]{:S(2)}) %all-to-all-start.2) | async-done | bytes 65568 | tf_op jit(solution)/shard_map/all_to_all | solution.py:562
  90.6 0.7 shard_map.65
  (1 shorter events, 0.0 us)
Async XLA Ops:
  0.6 13.7 %copy-start.1 = (bf16[3,9,36864]{2,0,1:T(4,128)(2,1)S(1)}, bf16[3,9,36864]{2,0,1:T(4,128)(2,1)}, u32[]{:S(2)}) copy-start(bf16[3,9,36864]{2,0,1:T(4,128)(2,1)} %param.5) | copy-start | bytes 5971972
  3.3 24.4 %all-to-all-start = ((bf16[16,288,128]{2,1,0:T(8,128)(2,1)}), bf16[16,288,128]{2,1,0:T(8,128)(2,1)}, u32[]{:S(2)}, u32[]{:S(2)}) async-start(bf16[16,288,128]{2,1,0:T(8,128)(2,1)} %shard_map.58), calls=%async_computation | async-start | bytes 2359296 | tf_op jit(solution)/shard_map/all_to_all | solution.py:69
  35.6 4.5 %collective-permute-start = (bf16[27,144,128]{2,1,0:T(8,128)(2,1)S(1)}, bf16[27,144,128]{2,1,0:T(8,128)(2,1)S(1)}, u32[]{:S(2)}, u32[]{:S(2)}) collective-permute-start(bf16[27,144,128]{2,1,0:T(8,128)(2,1)S(1)} %get-tuple-element.26), channel_id=1, source_target_pairs={{0,16},{16,0},{1,17},{17,1},{2,18},{18,2},{3,19},{19,3},{4,20},{20... | collective-permute-start | bytes 2985992 | tf_op jit(solution)/shard_map/ppermute | solution.py:543
  66.8 17.5 %copy-start = (bf16[1,16,9216]{2,1,0:T(8,128)(2,1)S(1)}, bf16[1,16,9216]{2,1,0:T(8,128)(2,1)}, u32[]{:S(2)}) copy-start(bf16[1,16,9216]{2,1,0:T(8,128)(2,1)} %x_ref.1) | copy-start | bytes 884740
  67.6 23.0 %all-to-all-start.2 = ((bf16[16,16,128]{2,1,0:T(8,128)(2,1)}), bf16[16,16,128]{2,1,0:T(8,128)(2,1)S(1)}, u32[]{:S(2)}, u32[]{:S(2)}) async-start(bf16[16,16,128]{2,1,0:T(8,128)(2,1)} %shard_map.64), calls=%async_computation.2 | async-start | bytes 131072 | tf_op jit(solution)/shard_map/all_to_all | solution.py:562
